TPU v7x, 32 devices: a whole 2x2x4 slice. The times are simulated.
32 devices in a mesh: section: 2 (over core), dp: 16 (over z, y, x).
Axes of the slice: x: 2, y: 2, z: 4, core: 2. Of those that a mesh axis runs over, the one named last changes fastest.
Arguments:
- boundary: bfloat16 [2, 2, 16, 128, 1024], P('section', None, 'dp'), may hold values from -8 to 8
- segments: int32 [2, 16, 128], P(None, 'dp'), may hold values from 0 to 3, never falling along the last dimension, each value on 1 to 64 neighbouring positions
- ln_gain: float32 [2, 1024], P('section', 'dp'), may hold values from 0.5 to 1.5
- ln_bias: float32 [2, 1024], P('section', 'dp'), may hold values from -1.75 to 1.75
- w_qkv: float32 [2, 1024, 3072], P('section', 'dp'), may hold values from -0.1875 to 0.1875
- w_out: float32 [2, 1024, 1024], P('section', 'dp'), may hold values from -0.75 to 0.75
- w_in: float32 [2, 1024, 4096], P('section', 'dp'), may hold values from -0.1875 to 0.1875
- b_in: float32 [2, 4096], P('section', 'dp'), may hold values from -3 to 3
- w_fc: float32 [2, 4096, 1024], P('section', 'dp'), may hold values from -0.09375 to 0.09375
- b_fc: float32 [2, 1024], P('section', 'dp'), may hold values from -1.75 to 1.75
Outputs:
- boundary_out: float32 [2, 2, 16, 128, 1024], P('section', None, 'dp')
- g_ln_gain: float32 [2, 1024], P('section', 'dp')
- g_ln_bias: float32 [2, 1024], P('section', 'dp')
- g_w_qkv: float32 [2, 1024, 3072], P('section', 'dp')
- g_w_out: float32 [2, 1024, 1024], P('section', 'dp')
- g_w_in: float32 [2, 1024, 4096], P('section', 'dp')
- g_b_in: float32 [2, 4096], P('section', 'dp')
- g_w_fc: float32 [2, 4096, 1024], P('section', 'dp')
- g_b_fc: float32 [2, 1024], P('section', 'dp')
Inputs may be any that keep to these rules, and one draw needn't show every extreme that they name: `segments`: in each row the ids never fall; each protein spans 1 to 64 tokens of its row.
All inputs are finite; a program needn't handle non-finite values.
Results may differ from a plain program's by a relative error of at most 0.012.
The roundings to bfloat16 on the way count: a program that leaves them out, or rounds other values in their place, can miss the bound.
Values may be sent and summed in bfloat16 or wider, within the bound.
No kernel may reach another device: no remote copies, remote signals or barrier semaphores. Data moves between devices by JAX's collectives and lax.ppermute only.
A program may use at most 256 MiB of HBM per device.

v0:
```python
import jax
import jax.numpy as jnp
from jax import lax
from jax.sharding import PartitionSpec as P

HEADS = 16
HEAD_DIM = 64
ROT = 32


EPSILON = 1e-05
NEGATIVE = -1000000000.0


def as_sent(x):

    def short(part):
        return part.astype(jnp.bfloat16) if part.dtype == jnp.float32 else part

    return jax.tree.map(short, x)


def shifted(value, axis, steps):
    count = lax.axis_size(axis)
    first, last = (max(0, -steps), min(count, count - steps))
    return lax.ppermute(value, axis, [(source, source + steps) for source in range(first, last)])


def positions_of(segments):
    last = segments.ndim - 1
    index = lax.broadcasted_iota(jnp.int32, segments.shape, last)
    previous = jnp.concatenate([segments[..., :1] - 1, segments[..., :-1]], axis=-1)
    starts = jnp.where(segments != previous, index, 0)
    return index - lax.cummax(starts, axis=last)


def angles_of(positions, rotary):
    freq = 10000.0 ** (-jnp.arange(0, rotary, 2).astype(jnp.float32) / rotary)
    angle = positions.astype(jnp.float32)[..., None] * freq
    return (jnp.cos(angle)[..., None, :], jnp.sin(angle)[..., None, :])


def allowed_of(segments):
    length = segments.shape[-1]
    row = lax.broadcasted_iota(jnp.int32, (length, length), 0)
    col = lax.broadcasted_iota(jnp.int32, (length, length), 1)
    same = segments[..., :, None] == segments[..., None, :]
    return (same & (col <= row))[..., None, :, :]


def rotate(values, cosine, sine):
    span = cosine.shape[-1] * 2
    first = values[..., 0:span:2]
    second = values[..., 1:span:2]
    turned = jnp.stack([first * cosine - second * sine, first * sine + second * cosine], axis=-1)
    turned = turned.reshape(values.shape[:-1] + (span,))
    return jnp.concatenate([turned, values[..., span:]], axis=-1)


def gelu(value):
    return 0.5 * value * (1.0 + jnp.tanh(0.7978845608 * (value + 0.044715 * value * value * value)))


def attention_scores(query, key, allowed):
    scores = jnp.einsum(
        "bqhe,bkhe->bhqk", query, key, preferred_element_type=jnp.float32
    ) * HEAD_DIM ** (-0.5)
    return jnp.where(allowed, scores, NEGATIVE)


def layer_forward(source, params, cosine, sine, allowed):
    gain, shift, w_qkv, w_out, w_in, b_in, w_fc, b_fc = params
    width = source.shape[-1]
    shape4 = source.shape[:2] + (HEADS, HEAD_DIM)
    mean = jnp.mean(source, -1, keepdims=True)
    centered = source - mean
    scale_inv = lax.rsqrt(jnp.mean(centered * centered, -1, keepdims=True) + EPSILON)
    unit = centered * scale_inv
    normed = (unit * gain.astype(jnp.float32) + shift.astype(jnp.float32)).astype(jnp.bfloat16)
    qkv = jnp.einsum("bld,de->ble", normed, w_qkv, preferred_element_type=jnp.float32)
    query = rotate(qkv[..., :width].reshape(shape4), cosine, sine).astype(jnp.bfloat16)
    key = rotate(qkv[..., width : 2 * width].reshape(shape4), cosine, sine).astype(jnp.bfloat16)
    value = qkv[..., 2 * width :].reshape(shape4).astype(jnp.bfloat16)
    scores = attention_scores(query, key, allowed)
    top = jnp.max(scores, -1, keepdims=True)
    expo = jnp.exp(scores - top)
    total = jnp.sum(expo, -1, keepdims=True)
    probs = (expo / total).astype(jnp.bfloat16)
    logsum = top + jnp.log(total)
    attended = jnp.einsum("bhqk,bkhe->bqhe", probs, value, preferred_element_type=jnp.float32)
    attended = attended.reshape(source.shape).astype(jnp.bfloat16)
    attention = jnp.einsum("bld,de->ble", attended, w_out, preferred_element_type=jnp.float32)
    pre = jnp.einsum("bld,df->blf", normed, w_in, preferred_element_type=jnp.float32) + b_in.astype(
        jnp.float32
    )
    active = gelu(pre).astype(jnp.bfloat16)
    mixed = jnp.einsum(
        "blf,fd->bld", active, w_fc, preferred_element_type=jnp.float32
    ) + b_fc.astype(jnp.float32)
    result = source + attention + mixed
    kept = (unit, scale_inv, normed, query, key, value, logsum, attended, pre, active)
    return (result, kept)


def layer_backward(incoming, kept, params, cosine, sine, allowed):
    gain, shift, w_qkv, w_out, w_in, b_in, w_fc, b_fc = params
    unit, scale_inv, normed, query, key, value, logsum, attended, pre, active = kept
    shape4 = incoming.shape[:2] + (HEADS, HEAD_DIM)
    flat = incoming.astype(jnp.float32)
    g_bfc = jnp.sum(flat, axis=(0, 1))
    g_wfc = jnp.einsum("blf,bld->fd", active, incoming, preferred_element_type=jnp.float32)
    g_active = jnp.einsum("bld,fd->blf", incoming, w_fc, preferred_element_type=jnp.float32)
    g_pre = jax.vjp(gelu, pre)[1](g_active)[0].astype(jnp.bfloat16)
    g_bin = jnp.sum(g_pre.astype(jnp.float32), axis=(0, 1))
    g_win = jnp.einsum("bld,blf->df", normed, g_pre, preferred_element_type=jnp.float32)
    g_normed = jnp.einsum("blf,df->bld", g_pre, w_in, preferred_element_type=jnp.float32)
    g_wout = jnp.einsum("bld,ble->de", attended, incoming, preferred_element_type=jnp.float32)
    g_att = jnp.einsum("ble,de->bld", incoming, w_out, preferred_element_type=jnp.float32)
    g_att = g_att.astype(jnp.bfloat16).reshape(shape4)
    probs = jnp.exp(attention_scores(query, key, allowed) - logsum)
    g_probs = jnp.einsum("bqhe,bkhe->bhqk", g_att, value, preferred_element_type=jnp.float32)
    g_value = jnp.einsum(
        "bhqk,bqhe->bkhe", probs.astype(jnp.bfloat16), g_att, preferred_element_type=jnp.float32
    )
    g_scores = probs * (g_probs - jnp.sum(g_probs * probs, -1, keepdims=True))
    g_scores = g_scores.astype(jnp.bfloat16)
    scale = HEAD_DIM ** (-0.5)
    g_query = (
        jnp.einsum("bhqk,bkhe->bqhe", g_scores, key, preferred_element_type=jnp.float32) * scale
    )
    g_key = (
        jnp.einsum("bhqk,bqhe->bkhe", g_scores, query, preferred_element_type=jnp.float32) * scale
    )
    g_query = rotate(g_query, cosine, -sine).reshape(incoming.shape)
    g_key = rotate(g_key, cosine, -sine).reshape(incoming.shape)
    g_qkv = jnp.concatenate([g_query, g_key, g_value.reshape(incoming.shape)], axis=-1).astype(
        jnp.bfloat16
    )
    g_wqkv = jnp.einsum("bld,ble->de", normed, g_qkv, preferred_element_type=jnp.float32)
    g_normed = (
        jnp.einsum("ble,de->bld", g_qkv, w_qkv, preferred_element_type=jnp.float32) + g_normed
    )
    g_gain = jnp.sum(g_normed * unit, axis=(0, 1))
    g_shift = jnp.sum(g_normed, axis=(0, 1))
    g_unit = g_normed * gain.astype(jnp.float32)
    g_source = scale_inv * (
        g_unit
        - jnp.mean(g_unit, -1, keepdims=True)
        - unit * jnp.mean(g_unit * unit, -1, keepdims=True)
    )
    grads = (g_gain, g_shift, g_wqkv, g_wout, g_win, g_bin, g_wfc, g_bfc)
    return (flat + g_source, grads)


def pick(array, index):
    return lax.dynamic_index_in_dim(array, index, 0, keepdims=False)


def body(boundary, segments, ln_gain, ln_bias, w_qkv, w_out, w_in, b_in, w_fc, b_fc):
    section = lax.axis_index("section")
    micro = boundary.shape[1]
    own = boundary[0]
    masters = (ln_gain, ln_bias, w_qkv, w_out, w_in, b_in, w_fc, b_fc)
    lowered = tuple((m.astype(jnp.bfloat16) for m in masters))
    gathered = jax.tree.map(
        lambda part, own: part.astype(own.dtype),
        lax.all_gather(as_sent(lowered), "dp", axis=1, tiled=True),
        lowered,
    )
    params = tuple((g[0] for g in gathered))
    cos_all, sin_all = angles_of(positions_of(segments), ROT)
    allow_all = allowed_of(segments)
    received = jnp.zeros_like(own[0])
    inputs, results, stores = ([], [], [])
    for step in range(micro + 1):
        index = jnp.clip(step - section, 0, micro - 1)
        source = jnp.where(section == 0, pick(own, index), received)
        result, kept = layer_forward(
            source.astype(jnp.float32),
            params,
            pick(cos_all, index),
            pick(sin_all, index),
            pick(allow_all, index),
        )
        inputs.append(source)
        results.append(result)
        stores.append(kept)
        if step < micro:
            received = shifted(result.astype(jnp.bfloat16), "section", 1)
    stacked_inputs = jnp.stack(inputs)
    returned = jnp.zeros_like(own[0])
    totals = tuple((jnp.zeros(p.shape, jnp.float32) for p in params))
    shards = tuple((jnp.zeros(m.shape, jnp.float32) for m in masters))
    back_results = []
    for step in range(micro + 1):
        raw = step - 1 + section
        valid = (raw >= 0) & (raw < micro)
        index = jnp.clip(raw, 0, micro - 1)
        anchor = jnp.clip(step - 1 + 2 * section, 0, micro)
        cosine, sine, allowed = (pick(cos_all, index), pick(sin_all, index), pick(allow_all, index))
        incoming = jnp.where(section == 1, pick(own, index), returned)
        kept = layer_forward(
            pick(stacked_inputs, anchor).astype(jnp.float32), params, cosine, sine, allowed
        )[1]
        g_source, grads = layer_backward(incoming, kept, params, cosine, sine, allowed)
        masked = tuple((jnp.where(valid, g, 0.0) for g in grads))
        totals = tuple((t + g for t, g in zip(totals, masked)))
        back_results.append(g_source)
        if step < micro:
            returned = shifted(g_source.astype(jnp.bfloat16), "section", -1)
    shards = lax.psum_scatter(
        tuple((t[None] for t in totals)), "dp", scatter_dimension=1, tiled=True
    )
    outputs = lax.dynamic_slice_in_dim(jnp.stack(results), section, micro, 0)
    gradients = lax.dynamic_slice_in_dim(jnp.stack(back_results), 1 - section, micro, 0)
    boundary_out = jnp.where(section == 0, gradients, outputs)[None]
    return (
        boundary_out,
        shards[0],
        shards[1],
        shards[2],
        shards[3],
        shards[4],
        shards[5],
        shards[6],
        shards[7],
    )


def solution(mesh):
    placed = (
        P("section", None, "dp", None, None),
        P(None, "dp", None),
        P("section", "dp"),
        P("section", "dp"),
        P("section", "dp", None),
        P("section", "dp", None),
        P("section", "dp", None),
        P("section", "dp"),
        P("section", "dp", None),
        P("section", "dp"),
    )
    return jax.shard_map(
        body,
        mesh=mesh,
        in_specs=placed,
        out_specs=(
            P("section", None, "dp", None, None),
            P("section", "dp"),
            P("section", "dp"),
            P("section", "dp", None),
            P("section", "dp", None),
            P("section", "dp", None),
            P("section", "dp"),
            P("section", "dp", None),
            P("section", "dp"),
        ),
        check_vma=False,
    )
```

profile of v0, /device:TPU:0, one launch (start us, length us, event | category | flops | bytes accessed | tf_op | source)
XLA Modules:
  0.0 1925.7 jit_solution(4992231983705060353)
XLA Ops:
  14.6 44.8 %all-reduce.3 = (bf16[1024]{0:T(1024)(128)(2,1)S(1)}, bf16[1024]{0:T(1024)(128)(2,1)S(1)}, bf16[1024]{0:T(1024)(128)(2,1)S(1)}) all-reduce(bf16[1024]{0:T(1024)(128)(2,1)S(1)} %dynamic-update-slice.2, bf16[1024]{0:T(1024)(128)(2,1)S(1)} %dynamic-update-slice.1, ...), channel_id=1, replica_groups=mesh['section'=2,'dp'=16] {'dp'}, use_global_device_ids=true, to_apply=%add.2 | all-reduce | flops 3072 | bytes 12288
  59.4 36.0 %all_gather.29 = bf16[1,4096]{1,0:T(2,128)(2,1)S(1)} all-gather(bf16[1,256]{1,0:T(2,128)(2,1)S(1)} %convert_element_type.686), channel_id=1, replica_groups=mesh['section'=2,'dp'=16] {'dp'}, dimensions={1}, use_global_device_ids=true | all-gather | bytes 8704 | tf_op jit(solution)/shard_map/all_gather | solution.py:167
  98.0 11.0 all-gather.5.cloned.1.call-done
  115.6 108.0 %all-gather.9.cloned.1.call-done = bf16[1,1024,4096]{2,1,0:T(8,128)(2,1)} async-done(((bf16[1,64,4096]{2,1,0:T(8,128)(2,1)}), bf16[1,1024,4096]{2,1,0:T(8,128)(2,1)}) %all-gather.9.cloned.1.call-update) | async-done | bytes 8388624 | tf_op jit(solution)/shard_map/all_gather | solution.py:167
  223.6 114.4 %all-gather.11.cloned.1.call-done = bf16[1,4096,1024]{2,1,0:T(8,128)(2,1)} async-done(((bf16[1,256,1024]{2,1,0:T(8,128)(2,1)}), bf16[1,4096,1024]{2,1,0:T(8,128)(2,1)}) %all-gather.11.cloned.1.call-update) | async-done | bytes 8388624 | tf_op jit(solution)/shard_map/all_gather | solution.py:167
  338.0 8.5 fusion.183
  346.5 53.6 %all-gather.7.cloned.1.call-done = bf16[1,1024,1024]{2,1,0:T(8,128)(2,1)} async-done(((bf16[1,64,1024]{2,1,0:T(8,128)(2,1)}), bf16[1,1024,1024]{2,1,0:T(8,128)(2,1)}) %all-gather.7.cloned.1.call-update) | async-done | bytes 2097168 | tf_op jit(solution)/shard_map/all_gather | solution.py:167
  406.3 3.9 fusion.72
  413.6 8.7 fusion.189
  521.8 4.9 fusion.57
  526.7 8.9 convert_reduce_fusion.2
  569.4 8.9 convert_reduce_fusion.1
  580.6 7.1 fusion.307
  607.5 7.8 convert_reduce_fusion
  617.6 7.2 fusion.327
  629.2 5.0 add_bitcast_fusion.3
  638.4 6.5 fusion.340
  644.9 8.8 add_bitcast_fusion.2
  655.2 8.2 fusion.228
  663.5 8.2 fusion.229
  671.6 11.2 add_bitcast_fusion
  684.0 8.3 fusion.587
  692.3 8.3 fusion.584
  700.6 11.2 add_bitcast_fusion.1
  720.4 9.5 fusion.195
  734.7 20.0 %reduce-scatter.25.cloned.1.call-done = f32[64,1]{1,0:T(8,128)} async-done(((f32[1024,1]{1,0:T(8,128)}), f32[64,1]{1,0:T(8,128)}) %reduce-scatter.25.cloned.1.call-update) | async-done | bytes 272
  756.0 73.8 %reduce-scatter.27.cloned.1.call-done = f32[64,1]{1,0:T(8,128)} async-done(((f32[1024,1]{1,0:T(8,128)}), f32[64,1]{1,0:T(8,128)}) %reduce-scatter.27.cloned.1.call-update) | async-done | bytes 272
  831.2 77.8 %reduce-scatter.29.cloned.1.call-done = f32[256,1]{1,0:T(8,128)} async-done(((f32[4096,1]{1,0:T(8,128)}), f32[256,1]{1,0:T(8,128)}) %reduce-scatter.29.cloned.1.call-update) | async-done | bytes 1040
  910.5 93.9 %reduce-scatter.19.cloned.1.call-done = f32[1,64,1024]{2,1,0:T(8,128)} async-done(((f32[1,1024,1024]{2,1,0:T(8,128)}), f32[1,64,1024]{2,1,0:T(8,128)}) %reduce-scatter.19.cloned.1.call-update) | async-done | bytes 262160 | tf_op jit(solution)/shard_map/reduce_scatter | solution.py:211
  1004.4 210.6 %reduce-scatter.17.cloned.1.call-done = f32[1,64,3072]{2,1,0:T(8,128)} async-done(((f32[1,1024,3072]{2,1,0:T(8,128)}), f32[1,64,3072]{2,1,0:T(8,128)}) %reduce-scatter.17.cloned.1.call-update) | async-done | bytes 786448 | tf_op jit(solution)/shard_map/reduce_scatter | solution.py:211
  1215.0 348.9 %reduce-scatter.23.cloned.1.call-done = f32[1,256,1024]{2,1,0:T(8,128)} async-done(((f32[1,4096,1024]{2,1,0:T(8,128)}), f32[1,256,1024]{2,1,0:T(8,128)}) %reduce-scatter.23.cloned.1.call-update) | async-done | bytes 1048592 | tf_op jit(solution)/shard_map/reduce_scatter | solution.py:211
  1563.9 354.8 %reduce-scatter.21.cloned.1.call-done = f32[1,64,4096]{2,1,0:T(8,128)} async-done(((f32[1,1024,4096]{2,1,0:T(8,128)}), f32[1,64,4096]{2,1,0:T(8,128)}) %reduce-scatter.21.cloned.1.call-update) | async-done | bytes 1048592 | tf_op jit(solution)/shard_map/reduce_scatter | solution.py:211
  (599 shorter events, 209.5 us)
Async XLA Ops:
  7.2 101.8 %all-gather.5.cloned.1.call-start = ((), (), s32[]{:S(2)}) async-start(), calls=%async_computation.8 | async-start | bytes 6684672 | tf_op jit(solution)/shard_map/all_gather | solution.py:167
  9.4 86.2 %copy-start.3 = (bf16[1,2,1,128,1024]{4,3,2,1,0:T(8,128)(2,1)S(1)}, bf16[1,2,1,128,1024]{4,3,2,1,0:T(8,128)(2,1)}, u32[]{:S(2)}) copy-start(bf16[1,2,1,128,1024]{4,3,2,1,0:T(8,128)(2,1)} %param.10) | copy-start | bytes 1572868
  9.4 214.2 %all-gather.9.cloned.1.call-start = ((), (), s32[]{:S(2)}) async-start(), calls=%async_computation.10 | async-start | bytes 8912896 | tf_op jit(solution)/shard_map/all_gather | solution.py:167
  10.4 327.6 %all-gather.11.cloned.1.call-start = ((), (), s32[]{:S(2)}) async-start(), calls=%async_computation.11 | async-start | bytes 8912896 | tf_op jit(solution)/shard_map/all_gather | solution.py:167
  11.3 388.8 %all-gather.7.cloned.1.call-start = ((), (), s32[]{:S(2)}) async-start(), calls=%async_computation.9 | async-start | bytes 2228224 | tf_op jit(solution)/shard_map/all_gather | solution.py:167
  12.1 721.3 %reduce-scatter.31.cloned.1.call-start = ((), (), s32[]{:S(2)}) async-start(), calls=%async_computation.19 | async-start | bytes 557056
  59.4 354.3 %copy-start.127 = (f32[1024]{0:T(1024)}, f32[1024]{0:T(1024)S(1)}, u32[]{:S(2)}) copy-start(f32[1024]{0:T(1024)S(1)} %convert_element_type.788) | copy-start | bytes 12292
  95.5 318.2 %copy-start.85 = (f32[1,4096]{1,0:T(1,128)}, f32[1,4096]{1,0:T(1,128)S(1)}, u32[]{:S(2)}) copy-start(f32[1,4096]{1,0:T(1,128)S(1)} %convert_element_type.781) | copy-start | bytes 49156
  97.0 422.3 %copy-start.89 = (f32[128,16]{0,1:T(8,128)}, f32[128,16]{0,1:T(8,128)S(1)}, u32[]{:S(2)}) copy-start(f32[128,16]{0,1:T(8,128)S(1)} %get-tuple-element.135) | copy-start | bytes 24580
  403.0 2.9 collective-permute-start
  406.0 16.3 copy-start.13
  424.7 3.8 collective-permute-start.1
  476.0 13.7 copy-start.131
  476.0 13.7 copy-start.106
  521.2 31.1 %copy-start.4 = (f32[16,128,128]{1,2,0:T(8,128)}, f32[16,128,128]{1,2,0:T(8,128)S(1)}, u32[]{:S(2)}) copy-start(f32[16,128,128]{1,2,0:T(8,128)S(1)} %get-tuple-element.177) | copy-start | bytes 3145732
  521.7 14.0 copy-start.42
  521.8 13.9 copy-start.44
  521.8 13.9 slice-start
  521.8 16.2 slice-start.6
  526.7 11.2 slice-start.7
  542.7 10.7 collective-permute-start.2
  564.4 13.9 slice-start.2
  580.6 9.5 copy-start.83
  588.8 4.0 collective-permute-start.3
  601.6 13.7 slice-start.4
  603.4 151.3 %reduce-scatter.25.cloned.1.call-start = ((), (), s32[]{:S(2)}) async-start(), calls=%async_computation.16 | async-start | bytes 557056
  625.9 204.0 %reduce-scatter.27.cloned.1.call-start = ((), (), s32[]{:S(2)}) async-start(), calls=%async_computation.17 | async-start | bytes 557056
  627.1 281.9 %reduce-scatter.29.cloned.1.call-start = ((), (), s32[]{:S(2)}) async-start(), calls=%async_computation.18 | async-start | bytes 2228224
  629.1 375.3 %reduce-scatter.19.cloned.1.call-start = ((), (), s32[]{:S(2)}) async-start(), calls=%async_computation.13 | async-start | bytes 4456448 | tf_op jit(solution)/shard_map/reduce_scatter | solution.py:211
  634.3 580.7 %reduce-scatter.17.cloned.1.call-start = ((), (), s32[]{:S(2)}) async-start(), calls=%async_computation.12 | async-start | bytes 13369344 | tf_op jit(solution)/shard_map/reduce_scatter | solution.py:211
  653.7 910.2 %reduce-scatter.23.cloned.1.call-start = ((), (), s32[]{:S(2)}) async-start(), calls=%async_computation.15 | async-start | bytes 17825792 | tf_op jit(solution)/shard_map/reduce_scatter | solution.py:211
  682.8 1235.8 %reduce-scatter.21.cloned.1.call-start = ((), (), s32[]{:S(2)}) async-start(), calls=%async_computation.14 | async-start | bytes 17825792 | tf_op jit(solution)/shard_map/reduce_scatter | solution.py:211
  (128 other events, 425.6 us)
Sparse Core Ops, SparseCore 0:
  11.4 97.5 all-gather.4
  112.3 111.2 all-gather.8
  226.9 111.0 all-gather.10
  341.2 58.8 all-gather.6
  603.6 75.8 reduce-scatter.30
  681.7 72.9 reduce-scatter.24
  756.9 72.8 reduce-scatter.26
  832.2 76.6 reduce-scatter.28
  911.9 92.4 reduce-scatter.18
  1011.5 203.4 reduce-scatter.16
  1217.9 345.9 reduce-scatter.22
  1566.6 351.9 reduce-scatter.20
where the time goes:
time: 1940 us; the launch traced here: 1930 us
  waiting for transfers between devices  1470 us (76%)
  matrix products  223 us (11%)
  local copies, waits for them, and re-layouts  101 us (5%)
  blocking collectives  80.8 us (4%)
  other arithmetic  29.2 us (2%)
    reduce_scatter x4, waiting for transfers between devices, body(): lax.psum_scatter(tuple((t[None] for t in totals)), 'dp', scatter_dimensio...  1010 us
    all_gather x4, waiting for transfers between devices, body(): lax.all_gather(as_sent(lowered), 'dp', axis=1, tiled=True)  287 us
    unnamed x16, waiting for transfers between devices  172 us
    unnamed x1, blocking collectives  44.8 us
  transfers between devices with their start and end apart: 16, of which 11 were waited for; matrix products, arithmetic and copies ran while one was open for 9% of the time, Pallas kernels for 0%

commit v1 on v0

v1 whole, which is shorter than its diff:
```python
import functools

import jax
import jax.numpy as jnp
from jax import lax
from jax.experimental import pallas as pl
from jax.experimental.pallas import tpu as pltpu
from jax.sharding import PartitionSpec as P

D = 1024
PAIR = 128
FB = 512
CI = 3 * PAIR + FB
RO = PAIR + FB
EPS = 1e-05
NEG = -1000000000.0
SCALE = 0.125
ROWS = 128
TOK = 4 * ROWS
BF = jnp.bfloat16
F32 = jnp.float32
VMEM_LIMIT = 56 * 1024 * 1024


def mm(a, b):
    return lax.dot_general(a, b, (((1,), (0,)), ((), ())), preferred_element_type=F32)


def mm_nt(a, b):
    return lax.dot_general(a, b, (((1,), (1,)), ((), ())), preferred_element_type=F32)


def mm_tn(a, b):
    return lax.dot_general(a, b, (((0,), (0,)), ((), ())), preferred_element_type=F32)


def gelu(h):
    return 0.5 * h * (1.0 + jnp.tanh(0.7978845608 * (h + 0.044715 * h * h * h)))


def gelu_slope(h):
    th = jnp.tanh(0.7978845608 * (h + 0.044715 * h * h * h))
    inner = 0.7978845608 * (1.0 + 3 * 0.044715 * h * h)
    return 0.5 * (1.0 + th) + 0.5 * h * (1.0 - th * th) * inner


def partner(x):
    lane = lax.broadcasted_iota(jnp.int32, x.shape, 1)
    return jnp.where(lane % 2 == 0, pltpu.roll(x, PAIR - 1, 1), pltpu.roll(x, 1, 1))


def turned(x, cosine, sine):
    return x * cosine + partner(x) * sine


def by_head(x):
    lane = lax.broadcasted_iota(jnp.int32, (1, PAIR), 1)
    low = jnp.where(lane < 64, 1.0, 0.0).astype(x.dtype)
    high = jnp.where(lane < 64, 0.0, 1.0).astype(x.dtype)
    return jnp.concatenate([x * low, x * high], axis=0)


def beside(x):
    return jnp.concatenate([x[:ROWS], x[ROWS:]], axis=1)


def rows_of(j):
    return pl.ds(j * ROWS, ROWS)


def layer_norm_into(x_refs, gain_ref, bias_ref, normed):
    for j, x_ref in enumerate(x_refs):
        x = x_ref[0:ROWS, :].astype(F32)
        centered = x - jnp.mean(x, -1, keepdims=True)
        inv = lax.rsqrt(jnp.mean(centered * centered, -1, keepdims=True) + EPS)
        normed[rows_of(j), :] = (centered * inv * gain_ref[...] + bias_ref[...]).astype(BF)


def forward_in(g, normed, wi, bin_ref, cos_ref, sin_ref, mask_ref, qkv, probs, oa, pre):
    y = mm(normed[...], wi[g, :, 0 : 3 * PAIR])
    cosine, sine = cos_ref[...], sin_ref[...]
    qkv[g, :, 0:PAIR] = turned(y[:, 0:PAIR], cosine, sine).astype(BF)
    qkv[g, :, PAIR : 2 * PAIR] = turned(y[:, PAIR : 2 * PAIR], cosine, sine).astype(BF)
    qkv[g, :, 2 * PAIR : 3 * PAIR] = y[:, 2 * PAIR : 3 * PAIR].astype(BF)
    for j in range(4):
        q = qkv[g, rows_of(j), 0:PAIR]
        k = qkv[g, rows_of(j), PAIR : 2 * PAIR]
        v = qkv[g, rows_of(j), 2 * PAIR : 3 * PAIR]
        s = mm_nt(by_head(q), k) * SCALE
        allowed = mask_ref[j]
        s = jnp.where(jnp.concatenate([allowed, allowed], axis=0) > 0.5, s, NEG)
        e = jnp.exp(s - jnp.max(s, -1, keepdims=True))
        p = e / jnp.sum(e, -1, keepdims=True)
        probs[g, j] = p
        oa[g, rows_of(j), 0:PAIR] = mm(beside(p.astype(BF)), by_head(v)).astype(BF)
    h = mm(normed[...], wi[g, :, 3 * PAIR : CI]) + bin_ref[g : g + 1, :]
    pre[g] = h
    oa[g, :, PAIR:RO] = gelu(h).astype(BF)


def forward_out(oa, wo, outs):
    for n in range(4):
        cols = slice(n * 256, (n + 1) * 256)
        part = mm(oa[0], wo[0, :, cols]) + mm(oa[1], wo[1, :, cols])
        for j in range(4):
            outs[j][:, cols] = part[j * ROWS : (j + 1) * ROWS].astype(outs[j].dtype)


def backward_out(g, gout, wo, qkv, probs, pre, cos_ref, sin_ref, gcat, gbin_ref):
    go = mm_nt(gout[...], wo[g, 0:PAIR, :]).astype(BF)
    for j in range(4):
        q = qkv[g, rows_of(j), 0:PAIR]
        k = qkv[g, rows_of(j), PAIR : 2 * PAIR]
        v = qkv[g, rows_of(j), 2 * PAIR : 3 * PAIR]
        cosine, sine = cos_ref[rows_of(j), :], sin_ref[rows_of(j), :]
        go2 = by_head(go[j * ROWS : (j + 1) * ROWS])
        p = probs[g, j]
        gp = mm_nt(go2, v)
        gs = (p * (gp - jnp.sum(gp * p, -1, keepdims=True))).astype(BF)
        gv = mm_tn(p.astype(BF), go2)
        gq = mm(beside(gs), by_head(k)) * SCALE
        gk = mm_tn(gs, by_head(q)) * SCALE
        gcat[g, rows_of(j), 0:PAIR] = turned(gq, cosine, -sine).astype(BF)
        gcat[g, rows_of(j), PAIR : 2 * PAIR] = turned(gk, cosine, -sine).astype(BF)
        gcat[g, rows_of(j), 2 * PAIR : 3 * PAIR] = gv.astype(BF)
    ga = mm_nt(gout[...], wo[g, PAIR:RO, :])
    gpre = (ga * gelu_slope(pre[g])).astype(BF)
    gcat[g, :, 3 * PAIR : CI] = gpre
    gbin_ref[g : g + 1, :] = jnp.sum(gpre.astype(F32), 0, keepdims=True)


def backward_in(gcat, wi, outs):
    for n in range(4):
        cols = slice(n * 256, (n + 1) * 256)
        part = mm_nt(gcat[0], wi[0, cols, :]) + mm_nt(gcat[1], wi[1, cols, :])
        for j in range(4):
            outs[j][:, cols] = part[j * ROWS : (j + 1) * ROWS].astype(outs[j].dtype)


def input_copies(fast, refs, wi, sems, place):
    if not fast:
        return [pltpu.make_async_copy(refs[0], wi, sems.at[0])]
    me, core = place
    copies = []
    for own in range(2):
        g = core if own == 0 else 1 - core
        for f, flip in enumerate((0, 8, 1, 9)):
            for j in range(4):
                source = jnp.bitwise_xor(me, flip ^ (2 * j))
                start = pl.multiple_of(source * 64, 64)
                copies.append(
                    pltpu.make_async_copy(
                        refs[own * 4 + f].at[j], wi.at[g, pl.ds(start, 64), :], sems.at[len(copies)]
                    )
                )
    return copies


def output_copies(fast, refs, wo, sems, place):
    if not fast:
        return [pltpu.make_async_copy(refs[0], wo, sems.at[0])]
    me, core = place
    copies = []
    for own in range(2):
        half = core if own == 0 else 1 - core
        for f, flip in enumerate((0, 8, 1, 9)):
            source = jnp.bitwise_xor(me, flip)
            g, r = source // 8, source % 2
            ref = refs[own * 4 + f]
            first = pl.multiple_of(64 * r + 32 * half, 32)
            second = pl.multiple_of(PAIR + 256 * r + 128 * half, 128)
            copies.append(
                pltpu.make_async_copy(ref.at[0:32], wo.at[g, pl.ds(first, 32), :], sems.at[len(copies)])
            )
            copies.append(
                pltpu.make_async_copy(ref.at[32:160], wo.at[g, pl.ds(second, 128), :], sems.at[len(copies)])
            )
    return copies


def place_of(fast):
    return (lax.axis_index("dp"), lax.axis_index("section")) if fast else None


def first_forward_kernel(fast, n_chunks, *refs):
    x_refs, refs = refs[:4], refs[4:]
    (gain, bias, bin_ref, cos_ref, sin_ref, mask_ref), refs = refs[:6], refs[6:]
    wi_refs, wo_refs, refs = refs[:n_chunks], refs[n_chunks : 2 * n_chunks], refs[2 * n_chunks :]
    outs, refs = refs[:4], refs[4:]
    normed, qkv, probs, oa, pre, wi, wo, sem_i, sem_o = refs
    place = place_of(fast)
    loads_i = input_copies(fast, wi_refs, wi, sem_i, place)
    loads_o = output_copies(fast, wo_refs, wo, sem_o, place)
    for copy in loads_i + loads_o:
        copy.start()
    layer_norm_into(x_refs, gain, bias, normed)
    for copy in loads_i:
        copy.wait()
    for g in range(2):
        forward_in(g, normed, wi, bin_ref, cos_ref, sin_ref, mask_ref, qkv, probs, oa, pre)
    for copy in loads_o:
        copy.wait()
    forward_out(oa, wo, outs)


def second_layer_kernel(fast, n_chunks, *refs):
    x_refs, gout_refs, refs = refs[:4], refs[4:8], refs[8:]
    (gain, bias, bin_ref, cos_ref, sin_ref, mask_ref), refs = refs[:6], refs[6:]
    wi_refs, wo_refs, refs = refs[:n_chunks], refs[n_chunks : 2 * n_chunks], refs[2 * n_chunks :]
    outs, gouts, refs = refs[:4], refs[4:8], refs[8:]
    normed, gcat, oa, gbin_ref, qkv, probs, pre, gout, wi, wo, sem_i, sem_o = refs
    place = place_of(fast)
    loads_i = input_copies(fast, wi_refs, wi, sem_i, place)
    loads_o = output_copies(fast, wo_refs, wo, sem_o, place)
    for copy in loads_i + loads_o:
        copy.start()
    layer_norm_into(x_refs, gain, bias, normed)
    for j in range(4):
        gout[rows_of(j), :] = gout_refs[j][ROWS : 2 * ROWS, :]
    for copy in loads_i:
        copy.wait()
    for g in range(2):
        forward_in(g, normed, wi, bin_ref, cos_ref, sin_ref, mask_ref, qkv, probs, oa, pre)
    for copy in loads_o:
        copy.wait()
    for g in range(2):
        backward_out(g, gout, wo, qkv, probs, pre, cos_ref, sin_ref, gcat, gbin_ref)
    backward_in(gcat, wi, gouts)
    forward_out(oa, wo, outs)


def first_backward_kernel(fast, n_chunks, *refs):
    gout_refs, refs = refs[:4], refs[4:]
    (cos_ref, sin_ref, qkv, probs, pre), refs = refs[:5], refs[5:]
    wi_refs, wo_refs, refs = refs[:n_chunks], refs[n_chunks : 2 * n_chunks], refs[2 * n_chunks :]
    gouts, refs = refs[:4], refs[4:]
    gcat, gbin_ref, gout, wi, wo, sem_i, sem_o = refs
    place = place_of(fast)
    loads_i = input_copies(fast, wi_refs, wi, sem_i, place)
    loads_o = output_copies(fast, wo_refs, wo, sem_o, place)
    for copy in loads_o + loads_i:
        copy.start()
    for j in range(4):
        gout[rows_of(j), :] = gout_refs[j][...]
    for copy in loads_o:
        copy.wait()
    for g in range(2):
        backward_out(g, gout, wo, qkv, probs, pre, cos_ref, sin_ref, gcat, gbin_ref)
    for copy in loads_i:
        copy.wait()
    backward_in(gcat, wi, gouts)


def weight_grad_out_kernel(fast, first, *refs):
    gout_refs, oa, refs = refs[:4], refs[4], refs[5:]
    *outs, gout = refs
    for j in range(4):
        gout[rows_of(j), :] = gout_refs[j][first : first + ROWS, :]
    if fast:
        keep, send = outs
        me, core = place_of(fast)
    for g in range(2):
        for r in range(2):
            small = mm_tn(oa[g, :, 64 * r : 64 * r + 64], gout[...]).astype(BF)
            large = mm_tn(oa[g, :, PAIR + 256 * r : PAIR + 256 * (r + 1)], gout[...]).astype(BF)
            if not fast:
                outs[0][g, 64 * r : 64 * r + 64, :] = small
                outs[0][g, PAIR + 256 * r : PAIR + 256 * (r + 1), :] = large
                continue
            flip = 2 * jnp.bitwise_xor(me % 2, r) + jnp.bitwise_xor(me // 8, g)

            @pl.when(core == 0)
            def _():
                keep[flip, 0:32, :], keep[flip, 32:160, :] = small[:32], large[:128]
                send[flip, 0:32, :], send[flip, 32:160, :] = small[32:], large[128:]

            @pl.when(core == 1)
            def _():
                keep[flip, 0:32, :], keep[flip, 32:160, :] = small[32:], large[128:]
                send[flip, 0:32, :], send[flip, 32:160, :] = small[:32], large[:128]


def weight_grad_in_kernel(fast, normed, gcat, *outs):
    if not fast:
        for g in range(2):
            for m in range(4):
                outs[0][g, m * 256 : (m + 1) * 256, :] = mm_tn(normed[:, m * 256 : (m + 1) * 256], gcat[g]).astype(BF)
        return
    me, core = place_of(fast)
    for own in (1, 0):
        g = core if own == 0 else 1 - core
        for m in range(4):
            part = mm_tn(normed[:, m * 256 : (m + 1) * 256], gcat[g]).astype(BF)
            for b in range(4):
                apart = jnp.bitwise_xor(me, 4 * m + b)
                flip, j = 2 * (apart % 2) + apart // 8, (apart // 2) % 4
                outs[own][flip, j] = part[64 * b : 64 * b + 64]


def norm_backward_kernel(own, r1, r2, r3, x_ref, gout_ref, gain, gx_ref, low_ref, sums_ref):
    x = x_ref[0:ROWS, :].astype(F32)
    gn = own[...] + r1[...].astype(F32) + r2[...].astype(F32) + r3[...].astype(F32)
    base = gout_ref.shape[0] - ROWS
    gout = gout_ref[base : base + ROWS, :].astype(F32)
    centered = x - jnp.mean(x, -1, keepdims=True)
    inv = lax.rsqrt(jnp.mean(centered * centered, -1, keepdims=True) + EPS)
    unit = centered * inv
    gu = gn * gain[...]
    gx = gout + inv * (gu - jnp.mean(gu, -1, keepdims=True) - unit * jnp.mean(gu * unit, -1, keepdims=True))
    gx_ref[...] = gx
    low_ref[...] = gx.astype(BF)
    sums_ref[0:1, :] = jnp.sum(gn * unit, 0, keepdims=True)
    sums_ref[1:2, :] = jnp.sum(gn, 0, keepdims=True)
    sums_ref[2:3, :] = jnp.sum(gout, 0, keepdims=True)


def pack_kernel(w_qkv, w_out, w_in, w_fc, wi_keep, wi_send, wo_keep, wo_send):
    t, core = (lax.axis_index("dp") // 2) % 4, lax.axis_index("section")
    for ref, g in ((wi_keep, core), (wi_send, 1 - core)):
        for j in range(4):
            rank = jnp.bitwise_xor(t, j)
            for part in range(3):
                start = pl.multiple_of(part * D + g * 512 + rank * PAIR, PAIR)
                ref[j, :, part * PAIR : (part + 1) * PAIR] = w_qkv[:, pl.ds(start, PAIR)].astype(BF)
            start = pl.multiple_of(g * 2048 + rank * FB, FB)
            ref[j, :, 3 * PAIR : CI] = w_in[:, pl.ds(start, FB)].astype(BF)
    for ref, half in ((wo_keep, core), (wo_send, 1 - core)):
        ref[0:32, :] = w_out[pl.ds(pl.multiple_of(32 * half, 32), 32), :].astype(BF)
        ref[32:160, :] = w_fc[pl.ds(pl.multiple_of(128 * half, 128), 128), :].astype(BF)


def unpack_kernel(own0, own1, own2, own3, other, wo_own, wo_other, g_qkv, g_out, g_in, g_fc):
    t, core = (lax.axis_index("dp") // 2) % 4, lax.axis_index("section")
    for side, g in ((0, core), (1, 1 - core)):
        for j in range(4):
            block = (own0, own1, own2, own3)[j][...] if side == 0 else other[j]
            block = block.astype(F32)
            rank = jnp.bitwise_xor(t, j)
            for part in range(3):
                start = pl.multiple_of(part * D + g * 512 + rank * PAIR, PAIR)
                g_qkv[:, pl.ds(start, PAIR)] = block[:, part * PAIR : (part + 1) * PAIR]
            start = pl.multiple_of(g * 2048 + rank * FB, FB)
            g_in[:, pl.ds(start, FB)] = block[:, 3 * PAIR : CI]
    for ref, half in ((wo_own, core), (wo_other, 1 - core)):
        g_out[pl.ds(pl.multiple_of(32 * half, 32), 32), :] = ref[0:32, :].astype(F32)
        g_fc[pl.ds(pl.multiple_of(128 * half, 128), 128), :] = ref[32:160, :].astype(F32)


VM = pl.BlockSpec(memory_space=pltpu.VMEM)
HB = pl.BlockSpec(memory_space=pl.ANY)


def kernel_call(kernel, args, outs, any_args=0, scratch=(), flops=1e6, name=None):
    sizes = [a.size * a.dtype.itemsize for a in args] + [a.size * a.dtype.itemsize for a in outs]
    return pl.pallas_call(
        kernel,
        out_shape=outs,
        in_specs=[VM] * (len(args) - any_args) + [HB] * any_args,
        out_specs=[VM] * len(outs),
        scratch_shapes=list(scratch),
        compiler_params=pltpu.CompilerParams(vmem_limit_bytes=VMEM_LIMIT),
        cost_estimate=pl.CostEstimate(flops=int(flops), bytes_accessed=int(sum(sizes)), transcendentals=0),
        name=name,
    )(*args)


def arr(shape, dtype):
    return jax.ShapeDtypeStruct(shape, dtype)


def weight_scratch(fast):
    return [
        pltpu.VMEM((2, D, CI), BF),
        pltpu.VMEM((2, RO, D), BF),
        pltpu.SemaphoreType.DMA((32 if fast else 1,)),
        pltpu.SemaphoreType.DMA((16 if fast else 1,)),
    ]


def partial_outs():
    return [arr((ROWS, D), F32)] + [arr((ROWS, D), BF)] * 3


def swap_core(value):
    return lax.ppermute(value, "section", [(0, 1), (1, 0)])


def flipped(value, flip, count):
    return lax.ppermute(value, "dp", [(i, i ^ flip) for i in range(count)])


def small_pack(gain, bias, b_fc, b_in):
    return jnp.concatenate([gain, bias, b_fc, b_in], axis=-1)


def body(boundary, segments, ln_gain, ln_bias, w_qkv, w_out, w_in, b_in, w_fc, b_fc):
    core, me = lax.axis_index("section"), lax.axis_index("dp")
    count = lax.axis_size("dp")
    fast = count == 16
    spread = count // 8
    rank = (me // spread) % 4
    steps = [j * spread for j in range(4)]
    first_core = core == 0
    share = D // count
    share_in = 4 * D // count
    width_small = 3 * share + share_in

    def across(values):
        return [flipped(v, steps[j + 1], count) for j, v in enumerate(values)]

    def choose(keep, recv):
        return jnp.where(first_core, keep, recv), jnp.where(first_core, recv, keep)

    swapped = swap_core(lax.dynamic_index_in_dim(boundary[0], 1 - core, 0, False)[0])
    kept = lax.dynamic_index_in_dim(boundary[0], core, 0, False)[0]
    x0, g1 = choose(kept, swapped)
    small = small_pack(ln_gain, ln_bias, b_fc, b_in).astype(BF)
    small0, small1 = choose(small, swap_core(small))
    seg = lax.dynamic_index_in_dim(segments, core, 0, False)[0].astype(BF)

    if fast:
        extra = jnp.concatenate(
            [
                jnp.pad(seg[None], ((0, 0), (0, D - ROWS))),
                jnp.pad(jnp.concatenate([small0, small1]), ((0, 13 + 0), (0, D - width_small))),
            ]
        )[:16]
    else:
        extra = jnp.zeros((16, D), BF).at[0, :ROWS].set(seg)
    pack = jnp.concatenate([x0, g1, extra])

    if fast:
        wi_keep, wi_send, wo_keep, wo_send = kernel_call(
            pack_kernel,
            [w_qkv[0], w_out[0], w_in[0], w_fc[0]],
            [arr((4, 64, CI), BF), arr((4, 64, CI), BF), arr((160, D), BF), arr((160, D), BF)],
            name="pack",
        )
        wi_recv, wo_recv = swap_core(wi_send), swap_core(wo_send)
        wi_first = [choose(wi_keep[j], wi_recv[j]) for j in range(4)]
        wo_first = choose(wo_keep, wo_recv)

        def gather(layer):
            mine = [w[layer] for w in wi_first]
            arrived = across(mine[1:])
            wi_own = jnp.stack([mine[0]] + arrived)
            wi_far = flipped(wi_own, 8, count)
            wi_got = [wi_own, wi_far, flipped(wi_own, 1, count), flipped(wi_far, 1, count)]
            wo_own = wo_first[layer]
            wo_far = flipped(wo_own, 8, count)
            wo_got = [wo_own, wo_far, flipped(wo_own, 1, count), flipped(wo_far, 1, count)]
            return wi_got + [swap_core(w) for w in wi_got], wo_got + [swap_core(w) for w in wo_got]

    else:
        t_groups = [
            [g * 4 * spread + t * spread + r for t in range(4)] for g in range(2) for r in range(spread)
        ]
        f_groups = [
            [g * 4 * spread + t * spread + r for g in range(2) for r in range(spread)] for t in range(4)
        ]
        wi = jnp.concatenate(
            [
                w_qkv[0].astype(BF).reshape(share, 3, 2, 4, PAIR).transpose(3, 0, 2, 1, 4).reshape(4, share, 2, 3 * PAIR),
                w_in[0].astype(BF).reshape(share, 2, 4, FB).transpose(2, 0, 1, 3),
            ],
            axis=-1,
        )
        wi = lax.all_to_all(wi, "dp", 0, 0, axis_index_groups=t_groups, tiled=True)
        wi = lax.all_gather(wi, "dp", axis_index_groups=f_groups)
        wi = wi.reshape(2, spread, 4, share, 2, CI).transpose(4, 0, 2, 1, 3, 5).reshape(2, D, CI)
        wo = lax.all_gather(w_out[0].astype(BF), "dp", axis_index_groups=f_groups).reshape(2, PAIR, D)
        wf = lax.all_gather(w_fc[0].astype(BF), "dp", axis_index_groups=f_groups).reshape(2, FB, D)
        wo = jnp.concatenate([wo, wf], axis=1)
        wi_both, wo_both = choose(wi, swap_core(wi)), choose(wo, swap_core(wo))

        def gather(layer):
            return [wi_both[layer]], [wo_both[layer]]

    n_chunks = 8 if fast else 1
    wi0, wo0 = gather(0)
    packs = [pack] + across([pack] * 3)
    wi1, wo1 = gather(1)

    if fast:
        held = jnp.stack([p[257:259, :width_small] for p in packs])
        held = jnp.concatenate([held, flipped(held, 8, count)])
        held = jnp.concatenate([held, flipped(held, 1, count)]).reshape(16, 2 * width_small)
        index = jnp.arange(16)
        flip_of = jnp.bitwise_xor(index, me)
        at = (flip_of % 2) * 8 + (flip_of // 8) * 4 + (flip_of // 2) % 4
        onehot = (at[:, None] == index[None, :]).astype(BF)
        everyone = mm(onehot, held).reshape(16, 2, width_small)
    else:
        everyone = lax.all_gather(jnp.concatenate([small0, small1]), "dp").astype(F32)

    def small_of(layer):
        one = everyone[:, layer]
        vectors = [one[:, i * share : (i + 1) * share].reshape(1, D) for i in range(3)]
        b = one[:, 3 * share :].reshape(2, 4, spread * share_in)
        b = lax.dynamic_index_in_dim(b, rank, 1, False)
        return vectors[0], vectors[1], vectors[2], b

    gain0, bias0, bfc0, bin0 = small_of(0)
    gain1, bias1, bfc1, bin1 = small_of(1)

    segs = jnp.stack([p[256, :ROWS] for p in packs])
    row = lax.broadcasted_iota(jnp.int32, (ROWS, ROWS), 0)
    col = lax.broadcasted_iota(jnp.int32, (ROWS, ROWS), 1)
    mask = ((segs[:, :, None] == segs[:, None, :]) & (col <= row)).astype(F32)
    positions = jnp.sum(mask, -1).reshape(TOK, 1) - 1.0
    lane = jnp.arange(PAIR) % 64
    freq = jnp.where(lane < 32, 10000.0 ** (-(lane // 2 * 2).astype(F32) / 32), 0.0)
    angle = positions * freq
    cosine = jnp.cos(angle)
    sine = jnp.sin(angle) * jnp.where(lane % 2 == 0, -1.0, 1.0)

    layer_flops = 2 * TOK * 2 * (D * CI + RO * D)
    saved = [
        arr((TOK, D), BF),
        arr((2, TOK, 3 * PAIR), BF),
        arr((2, 4, 2 * ROWS, ROWS), F32),
        arr((2, TOK, RO), BF),
        arr((2, TOK, FB), F32),
    ]
    got = kernel_call(
        functools.partial(first_forward_kernel, fast, n_chunks),
        [*packs, gain0, bias0, bin0, cosine, sine, mask, *wi0, *wo0],
        partial_outs() + saved,
        any_args=2 * n_chunks,
        scratch=weight_scratch(fast),
        flops=layer_flops,
        name="first_forward",
    )
    own, sends, (normed0, qkv0, probs0, oa0, pre0) = got[0], got[1:4], got[4:]

    def total(own, sends):
        return sum([r.astype(F32) for r in across(sends)], own)

    x1 = (x0.astype(F32) + total(own, sends) + bfc0).astype(BF)
    x1s = [x1] + across([x1] * 3)

    got = kernel_call(
        functools.partial(second_layer_kernel, fast, n_chunks),
        [*x1s, *packs, gain1, bias1, bin1, cosine, sine, mask, *wi1, *wo1],
        partial_outs()
        + partial_outs()
        + [arr((TOK, D), BF), arr((2, TOK, CI), BF), arr((2, TOK, RO), BF), arr((2, FB), F32)],
        any_args=2 * n_chunks,
        scratch=[
            pltpu.VMEM((2, TOK, 3 * PAIR), BF),
            pltpu.VMEM((2, 4, 2 * ROWS, ROWS), F32),
            pltpu.VMEM((2, TOK, FB), F32),
            pltpu.VMEM((TOK, D), BF),
        ]
        + weight_scratch(fast),
        flops=2 * layer_flops,
        name="second_layer",
    )
    out_own, out_sends, gn_own, gn_sends = got[0], got[1:4], got[4], got[5:8]
    normed1, gcat1, oa1, gbin1 = got[8:]

    def norm_backward(own, arrived, x, gout, gain, name):
        return kernel_call(
            norm_backward_kernel,
            [own, *arrived, x, gout, gain],
            [arr((ROWS, D), F32), arr((ROWS, D), BF), arr((3, D), F32)],
            name=name,
        )

    _, g0, sums1 = norm_backward(gn_own, across(gn_sends), x1, g1, gain1, "norm_backward1")
    g0s = [g0] + across([g0] * 3)
    out1 = x1.astype(F32) + total(out_own, out_sends) + bfc1

    def weight_grads(gouts, first, oa, normed, gcat, name):
        if fast:
            outs_o = [arr((4, 160, D), BF)] * 2
            outs_i = [arr((4, 4, 64, CI), BF)] * 2
        else:
            outs_o, outs_i = [arr((2, RO, D), BF)], [arr((2, D, CI), BF)]
        go = kernel_call(
            functools.partial(weight_grad_out_kernel, fast, first),
            [*gouts, oa],
            outs_o,
            scratch=[pltpu.VMEM((TOK, D), BF)],
            flops=2 * TOK * 2 * RO * D,
            name=name + "_out",
        )
        gi = kernel_call(
            functools.partial(weight_grad_in_kernel, fast),
            [normed, gcat],
            outs_i,
            flops=2 * TOK * 2 * CI * D,
            name=name + "_in",
        )
        return go, gi

    def reduce_over_f(keep, send):
        arrived = swap_core(send)
        both = keep.astype(F32) + arrived.astype(F32)
        near = flipped(both[2:4].astype(BF), 1, count)
        both = both[0:2] + near.astype(F32)
        far = flipped(both[1].astype(BF), 8, count)
        return both[0] + far.astype(F32)

    def reduce_fast(grads):
        go, gi = grads
        wo = reduce_over_f(*go)
        wi = reduce_over_f(*gi)
        parts = [wi[0].astype(BF)] + across([wi[j].astype(BF) for j in range(1, 4)])
        return wo.astype(BF), parts

    grads1 = weight_grads(packs, ROWS, oa1, normed1, gcat1, "grads1")

    got = kernel_call(
        functools.partial(first_backward_kernel, fast, n_chunks),
        [*g0s, cosine, sine, qkv0, probs0, pre0, *wi0, *wo0],
        partial_outs() + [arr((2, TOK, CI), BF), arr((2, FB), F32)],
        any_args=2 * n_chunks,
        scratch=[pltpu.VMEM((TOK, D), BF)] + weight_scratch(fast),
        flops=layer_flops,
        name="first_backward",
    )
    gn_own, gn_sends, gcat0, gbin0 = got[0], got[1:4], got[4], got[5]
    grads0 = weight_grads(g0s, 0, oa0, normed0, gcat0, "grads0")
    gx0, _, sums0 = norm_backward(gn_own, across(gn_sends), x0, g0, gain0, "norm_backward0")

    arrived = swap_core(jnp.where(first_core, out1, gx0))
    boundary_out = jnp.where(
        first_core, jnp.stack([gx0, arrived]), jnp.stack([arrived, out1])
    )[None, :, None]

    def small_grads(sums, gbin):
        vectors = sums.reshape(3, count, share).transpose(1, 0, 2).reshape(count, 3 * share)
        onehot = (jnp.arange(4) == rank).astype(F32)
        b = gbin.reshape(2, 1, spread, share_in) * onehot[None, :, None, None]
        return jnp.concatenate([vectors, b.reshape(count, share_in)], axis=1)

    both = choose(small_grads(sums0, gbin0), small_grads(sums1, gbin1))
    vector = both[0] + swap_core(both[1])
    if fast:
        for flip in (2, 4, 1, 8):
            vector = vector + flipped(vector, flip, count)
        vector = lax.dynamic_index_in_dim(vector, me, 0, True)
    else:
        vector = lax.psum_scatter(vector, "dp", scatter_dimension=0, tiled=True)
    g_gain, g_bias, g_bfc = (vector[:, i * share : (i + 1) * share] for i in range(3))
    g_bin = vector[:, 3 * share :]

    if fast:
        wo_1, wi_1 = reduce_fast(grads1)
        wo_0, wi_0 = reduce_fast(grads0)
        wo_mine, wo_theirs = choose(wo_0, wo_1)
        pairs = [choose(a, b) for a, b in zip(wi_0, wi_1)]
        wi_other = swap_core(jnp.stack([p[1] for p in pairs]))
        g_qkv, g_out, g_in, g_fc = kernel_call(
            unpack_kernel,
            [*[p[0] for p in pairs], wi_other, wo_mine, swap_core(wo_theirs)],
            [arr((64, 3 * D), F32), arr((64, D), F32), arr((64, 4 * D), F32), arr((256, D), F32)],
            name="unpack",
        )
    else:
        (go1,), (gi1,) = grads1
        (go0,), (gi0,) = grads0
        mine, theirs = choose(gi0, gi1)
        gi = mine.astype(F32) + swap_core(theirs).astype(F32)
        mine, theirs = choose(go0, go1)
        go = mine.astype(F32) + swap_core(theirs).astype(F32)
        gi = gi.reshape(2, 2, 4, spread, share, CI).transpose(1, 3, 2, 4, 0, 5).reshape(2 * spread, 4, share, 2, CI)
        gi = lax.psum_scatter(gi, "dp", scatter_dimension=0, axis_index_groups=f_groups)
        gi = lax.all_to_all(gi, "dp", 0, 0, axis_index_groups=t_groups, tiled=True)
        g_qkv = gi[..., : 3 * PAIR].reshape(4, share, 2, 3, PAIR).transpose(1, 3, 2, 0, 4).reshape(share, 3 * D)
        g_in = gi[..., 3 * PAIR :].transpose(1, 2, 0, 3).reshape(share, 4 * D)
        g_out = lax.psum_scatter(
            go[:, :PAIR].reshape(2 * spread, share, D), "dp", scatter_dimension=0, axis_index_groups=f_groups
        )
        g_fc = lax.psum_scatter(
            go[:, PAIR:].reshape(2 * spread, share_in, D), "dp", scatter_dimension=0, axis_index_groups=f_groups
        )

    return (boundary_out, g_gain, g_bias, g_qkv[None], g_out[None], g_in[None], g_bin, g_fc[None], g_bfc)


def solution(mesh):
    rows = P("section", None, "dp", None, None)
    vector, matrix = P("section", "dp"), P("section", "dp", None)
    return jax.shard_map(
        body,
        mesh=mesh,
        in_specs=(rows, P(None, "dp", None), vector, vector, matrix, matrix, matrix, vector, matrix, vector),
        out_specs=(rows, vector, vector, matrix, matrix, matrix, vector, matrix, vector),
        check_vma=False,
    )
```

time: 1940 us -> 456 us (0.24)
  waiting for transfers between devices: 1470 us -> 254 us
  matrix products: 223 us -> 0.19 us
  Pallas kernels: 0 us -> 82.9 us
  local copies, waits for them, and re-layouts: 101 us -> 20.1 us
  blocking collectives: 80.8 us -> 0 us
  starting transfers between devices: 7.58 us -> 70.3 us
    reduce_scatter x4 -> x0, waiting for transfers between devices: 1010 us -> none  [body(): lax.psum_scatter(tuple((t[None] for t in totals)), 'dp', scatter_dimensio...]
    all_gather x4 -> x0, waiting for transfers between devices: 287 us -> none  [body(): lax.all_gather(as_sent(lowered), 'dp', axis=1, tiled=True)]
    ppermute x4 -> x87, waiting for transfers between devices: 0.01 us -> 254 us  [the longest x59 252 us: flipped(): return lax.ppermute(value, 'dp', [(i, i ^ flip) for i in range(count)])]
    dot_general x60 -> x1, matrix products: 221 us -> 0.19 us  [mm(): lax.dot_general(a, b, (((1,), (0,)), ((), ())), preferred_element_type=F32)]
    unnamed x16 -> x0, waiting for transfers between devices: 172 us -> none
    pallas_call x0 -> x11, Pallas kernels: none -> 82.9 us  [kernel_call(): pl.pallas_call(kernel, out_shape=outs, in_specs=[VM] * (len(args) - any_a...]
    ppermute x4 -> x87, starting transfers between devices: 6.29 us -> 70.3 us  [the longest x59 65.3 us: flipped(): return lax.ppermute(value, 'dp', [(i, i ^ flip) for i in range(count)])]
    slice x72 -> x12, local copies, waits for them, and re-layouts: 63.8 us -> 3.87 us  [the longest x3 1.97 us: body(): segs = jnp.stack([p[256, :ROWS] for p in packs])]
  transfers between devices with their start and end apart: 16 -> 87, of which waited for: 11 -> 34; matrix products, arithmetic and copies ran while one was open for 9% -> 8% of each run, Pallas kernels for 0% -> 13%
where the time goes in v1:
time: 456 us; the launch traced here: 452 us
  waiting for transfers between devices  254 us (56%)
  Pallas kernels  82.9 us (18%)
  starting transfers between devices  70.3 us (15%)
  other arithmetic  22.7 us (5%)
  local copies, waits for them, and re-layouts  20.1 us (4%)
    ppermute x59, waiting for transfers between devices, flipped(): return lax.ppermute(value, 'dp', [(i, i ^ flip) for i in range(count)])  252 us
    pallas_call x11, Pallas kernels, kernel_call(): pl.pallas_call(kernel, out_shape=outs, in_specs=[VM] * (len(args) - any_a...  82.9 us
    ppermute x59, starting transfers between devices, flipped(): return lax.ppermute(value, 'dp', [(i, i ^ flip) for i in range(count)])  65.3 us
  transfers between devices with their start and end apart: 87, of which 34 were waited for; matrix products, arithmetic and copies ran while one was open for 8% of the time, Pallas kernels for 13%

profile of v1, /device:TPU:0, one launch (start us, length us, event | category | flops | bytes accessed | tf_op | source)
XLA Modules:
  0.0 451.9 jit_solution(12901461876674044934)
XLA Ops:
  5.0 3.2 pack.1
  22.8 23.9 %collective-permute-done.10 = bf16[64,896]{1,0:T(8,128)(2,1)S(1)} collective-permute-done((bf16[64,896]{1,0:T(8,128)(2,1)}, bf16[64,896]{1,0:T(8,128)(2,1)S(1)}, u32[]{:S(2)}, u32[]{:S(2)}) %collective-permute-start.10) | collective-permute-done | bytes 114720 | tf_op jit(solution)/shard_map/ppermute | solution.py:389
  52.1 3.2 collective-permute-done.34
  73.8 33.5 %collective-permute-done.5 = bf16[4,2,448]{2,1,0:T(2,128)(2,1)S(1)} collective-permute-done((bf16[4,2,448]{2,1,0:T(2,128)(2,1)S(1)}, bf16[4,2,448]{2,1,0:T(2,128)(2,1)S(1)}, u32[]{:S(2)}, u32[]{:S(2)}) %collective-permute-start.5) | collective-permute-done | bytes 7200 | tf_op jit(solution)/shard_map/ppermute | solution.py:389
  111.7 9.0 %collective-permute-done.6 = bf16[8,2,448]{2,1,0:T(2,128)(2,1)S(1)} collective-permute-done((bf16[8,2,448]{2,1,0:T(2,128)(2,1)S(1)}, bf16[8,2,448]{2,1,0:T(2,128)(2,1)S(1)}, u32[]{:S(2)}, u32[]{:S(2)}) %collective-permute-start.6) | collective-permute-done | bytes 14368 | tf_op jit(solution)/shard_map/ppermute | solution.py:389
  125.0 15.1 %collective-permute-done.21.refs_21_.refs_20_ = bf16[160,1024]{1,0:T(8,128)(2,1)S(1)} collective-permute-done((bf16[160,1024]{1,0:T(8,128)(2,1)}, bf16[160,1024]{1,0:T(8,128)(2,1)S(1)}, u32[]{:S(2)}, u32[]{:S(2)}) %collective-permute-start.21) | collective-permute-done | bytes 327712 | tf_op jit(solution)/shard_map/ppermute | solution.py:389
  140.2 3.6 collective-permute-done.35.refs_15_
  149.2 11.9 %first_forward.1 = (f32[128,1024]{1,0:T(8,128)}, bf16[128,1024]{1,0:T(8,128)(2,1)}, bf16[128,1024]{1,0:T(8,128)(2,1)}, bf16[128,1024]{1,0:T(8,128)(2,1)}, bf16[5...) custom-call(bf16[272,1024]{1,0:T(8,128)(2,1)} %copy-done.9, ...), custom_call_target="tpu_custom_call" | custom-call | flops 3221225472 | bytes 16920576 | tf_op jit(solution)/shard_map/first_forward/pallas_call | solution.py:355
  162.0 11.9 %collective-permute-done.44.refs_25_ = bf16[160,1024]{1,0:T(8,128)(2,1)} collective-permute-done((bf16[160,1024]{1,0:T(8,128)(2,1)}, bf16[160,1024]{1,0:T(8,128)(2,1)}, u32[]{:S(2)}, u32[]{:S(2)}) %collective-permute-start.44) | collective-permute-done | bytes 327712 | tf_op jit(solution)/shard_map/ppermute | solution.py:389
  175.2 7.2 %collective-permute-done.28 = bf16[128,1024]{1,0:T(8,128)(2,1)S(1)} collective-permute-done((bf16[128,1024]{1,0:T(8,128)(2,1)}, bf16[128,1024]{1,0:T(8,128)(2,1)S(1)}, u32[]{:S(2)}, u32[]{:S(2)}) %collective-permute-start.28) | collective-permute-done | bytes 262176 | tf_op jit(solution)/shard_map/ppermute | solution.py:389
  189.4 4.5 collective-permute-done.31.refs_3_
  193.9 4.0 collective-permute-done.30.refs_2_
  199.8 19.4 %second_layer.1 = (f32[128,1024]{1,0:T(8,128)}, bf16[128,1024]{1,0:T(8,128)(2,1)}, bf16[128,1024]{1,0:T(8,128)(2,1)}, bf16[128,1024]{1,0:T(8,128)(2,1)}, f32[128...) custom-call(bf16[128,1024]{1,0:T(8,128)(2,1)} %copy-done.2, ...), custom_call_target="tpu_custom_call" | custom-call | flops 6442450944 | bytes 17186816 | tf_op jit(solution)/shard_map/second_layer/pallas_call | solution.py:355
  222.8 5.0 %collective-permute-done.49.r1 = bf16[128,1024]{1,0:T(8,128)(2,1)S(1)} collective-permute-done((bf16[128,1024]{1,0:T(8,128)(2,1)}, bf16[128,1024]{1,0:T(8,128)(2,1)S(1)}, u32[]{:S(2)}, u32[]{:S(2)}) %collective-permute-start.49) | collective-permute-done | bytes 262176 | tf_op jit(solution)/shard_map/ppermute | solution.py:389
  229.4 5.1 %collective-permute-done.51.r3 = bf16[128,1024]{1,0:T(8,128)(2,1)S(1)} collective-permute-done((bf16[128,1024]{1,0:T(8,128)(2,1)}, bf16[128,1024]{1,0:T(8,128)(2,1)S(1)}, u32[]{:S(2)}, u32[]{:S(2)}) %collective-permute-start.51) | collective-permute-done | bytes 262176 | tf_op jit(solution)/shard_map/ppermute | solution.py:389
  243.1 5.4 %collective-permute-done.54.refs_3_ = bf16[128,1024]{1,0:T(8,128)(2,1)S(1)} collective-permute-done((bf16[128,1024]{1,0:T(8,128)(2,1)}, bf16[128,1024]{1,0:T(8,128)(2,1)S(1)}, u32[]{:S(2)}, u32[]{:S(2)}) %collective-permute-start.54) | collective-permute-done | bytes 262176 | tf_op jit(solution)/shard_map/ppermute | solution.py:389
  248.5 4.5 %collective-permute-done.53.refs_2_ = bf16[128,1024]{1,0:T(8,128)(2,1)S(1)} collective-permute-done((bf16[128,1024]{1,0:T(8,128)(2,1)}, bf16[128,1024]{1,0:T(8,128)(2,1)S(1)}, u32[]{:S(2)}, u32[]{:S(2)}) %collective-permute-start.53) | collective-permute-done | bytes 262176 | tf_op jit(solution)/shard_map/ppermute | solution.py:389
  253.8 15.6 %first_backward.1 = (f32[128,1024]{1,0:T(8,128)}, bf16[128,1024]{1,0:T(8,128)(2,1)}, bf16[128,1024]{1,0:T(8,128)(2,1)}, bf16[128,1024]{1,0:T(8,128)(2,1)}, bf16[...) custom-call(bf16[128,1024]{1,0:T(8,128)(2,1)} %get-tuple-element.68.refs_0_.gout_ref, bf16[128,1024]{1,0:T(8,128)(2,1)} %copy-done.42, ...), custom_call_target="tpu_custom_call" | custom-call | flops 3221225472 | bytes 14946304 | tf_op jit(solution)/shard_map/first_backward/pallas_call | solution.py:355
  273.0 6.5 %grads1_out.1 = (bf16[4,160,1024]{2,1,0:T(8,128)(2,1)}, bf16[4,160,1024]{2,1,0:T(8,128)(2,1)}) custom-call(bf16[272,1024]{1,0:T(8,128)(2,1)} %copy-done.9, bf16[272,1024]{1,0:T(8,128)(2,1)} %collective-permute-done.2.refs_1_.refs_5_, bf16[272,1024]{1,0:T(8,128)(2,1)} %collective-permute-done.3.refs_2_.refs_6_, ...), custom_call_target="tpu_custom_call" | custom-call | flops 1342177280 | bytes 6160384 | tf_op jit(solution)/shard_map/grads1_out/pallas_call | solution.py:355
  280.0 3.6 collective-permute-done.57.r3
  288.2 5.5 %grads1_in.1 = (bf16[4,4,64,896]{3,2,1,0:T(8,128)(2,1)}, bf16[4,4,64,896]{3,2,1,0:T(8,128)(2,1)}) custom-call(bf16[512,1024]{1,0:T(8,128)(2,1)} %get-tuple-element.89.normed, bf16[2,512,896]{2,1,0:T(8,128)(2,1)} %get-tuple-element.90.gcat), custom_call_target="tpu_custom_call" | custom-call | flops 1879048192 | bytes 6553600 | tf_op jit(solution)/shard_map/grads1_in/pallas_call | solution.py:355
  294.7 6.3 %grads0_out.1 = (bf16[4,160,1024]{2,1,0:T(8,128)(2,1)}, bf16[4,160,1024]{2,1,0:T(8,128)(2,1)}) custom-call(bf16[128,1024]{1,0:T(8,128)(2,1)} %get-tuple-element.68.refs_0_.gout_ref, bf16[128,1024]{1,0:T(8,128)(2,1)} %copy-done.42, bf16[128,1024]{1,0:T(8,128)(2,1)} %copy-done.41, bf16[128,1024]{1,0:T(8,128)(2,1)} %copy-done.40, ...), custom_call_target="tpu_custom_call" | custom-call | flops 1342177280 | bytes 4980736 | tf_op jit(solution)/shard_map/grads0_out/pallas_call | solution.py:355
  301.8 5.5 %grads0_in.1 = (bf16[4,4,64,896]{3,2,1,0:T(8,128)(2,1)}, bf16[4,4,64,896]{3,2,1,0:T(8,128)(2,1)}) custom-call(bf16[512,1024]{1,0:T(8,128)(2,1)} %get-tuple-element.85.normed, bf16[2,512,896]{2,1,0:T(8,128)(2,1)} %get-tuple-element.86.gcat), custom_call_target="tpu_custom_call" | custom-call | flops 1879048192 | bytes 6553600 | tf_op jit(solution)/shard_map/grads0_in/pallas_call | solution.py:355
  308.2 3.4 collective-permute-done.65
  314.0 6.1 %collective-permute-done.60 = bf16[128,1024]{1,0:T(8,128)(2,1)} collective-permute-done((bf16[128,1024]{1,0:T(8,128)(2,1)}, bf16[128,1024]{1,0:T(8,128)(2,1)}, u32[]{:S(2)}, u32[]{:S(2)}) %collective-permute-start.60) | collective-permute-done | bytes 262176 | tf_op jit(solution)/shard_map/ppermute | solution.py:389
  337.0 8.1 %collective-permute-done.84 = bf16[2,160,1024]{2,1,0:T(8,128)(2,1)S(1)} collective-permute-done((bf16[2,160,1024]{2,1,0:T(8,128)(2,1)S(1)}, bf16[2,160,1024]{2,1,0:T(8,128)(2,1)S(1)}, u32[]{:S(2)}, u32[]{:S(2)}) %collective-permute-start.84) | collective-permute-done | bytes 655392 | tf_op jit(solution)/shard_map/ppermute | solution.py:389
  346.5 32.4 %collective-permute-done.71 = bf16[2,4,64,896]{3,2,1,0:T(8,128)(2,1)S(1)} collective-permute-done((bf16[2,4,64,896]{3,2,1,0:T(8,128)(2,1)S(1)}, bf16[2,4,64,896]{3,2,1,0:T(8,128)(2,1)S(1)}, u32[]{:S(2)}, u32[]{:S(2)}) %collective-permute-start.71) | collective-permute-done | bytes 917536 | tf_op jit(solution)/shard_map/ppermute | solution.py:389
  380.2 17.9 %collective-permute-done.68 = bf16[2,4,64,896]{3,2,1,0:T(8,128)(2,1)S(1)} collective-permute-done((bf16[2,4,64,896]{3,2,1,0:T(8,128)(2,1)S(1)}, bf16[2,4,64,896]{3,2,1,0:T(8,128)(2,1)S(1)}, u32[]{:S(2)}, u32[]{:S(2)}) %collective-permute-start.68) | collective-permute-done | bytes 917536 | tf_op jit(solution)/shard_map/ppermute | solution.py:389
  401.7 19.5 %collective-permute-done.69 = bf16[4,64,896]{2,1,0:T(8,128)(2,1)S(1)} collective-permute-done((bf16[4,64,896]{2,1,0:T(8,128)(2,1)S(1)}, bf16[4,64,896]{2,1,0:T(8,128)(2,1)S(1)}, u32[]{:S(2)}, u32[]{:S(2)}) %collective-permute-start.69) | collective-permute-done | bytes 458784 | tf_op jit(solution)/shard_map/ppermute | solution.py:389
  424.3 5.1 %collective-permute-done.76 = bf16[64,896]{1,0:T(8,128)(2,1)S(1)} collective-permute-done((bf16[64,896]{1,0:T(8,128)(2,1)S(1)}, bf16[64,896]{1,0:T(8,128)(2,1)S(1)}, u32[]{:S(2)}, u32[]{:S(2)}) %collective-permute-start.76) | collective-permute-done | bytes 114720 | tf_op jit(solution)/shard_map/ppermute | solution.py:389
  439.0 3.3 collective-permute-done.78
  448.4 3.3 unpack.1
  (357 shorter events, 137.5 us)
Async XLA Ops:
  17.1 39.7 %collective-permute-start.4 = (bf16[272,1024]{1,0:T(8,128)(2,1)S(1)}, bf16[272,1024]{1,0:T(8,128)(2,1)}, u32[]{:S(2)}, u32[]{:S(2)}) collective-permute-start(bf16[272,1024]{1,0:T(8,128)(2,1)S(1)} %fusion.10.refs_0_.refs_4_), channel_id=1, source_target_pairs={{0,6},{1,7},{2,4},{3,5},{4,2},{5,3},{6,0},{7,1},{8,14},{9,15},{10,... | collective-permute-start | bytes 1671176 | tf_op jit(solution)/shard_map/ppermute | solution.py:389
  17.2 43.0 %collective-permute-start.3 = (bf16[272,1024]{1,0:T(8,128)(2,1)S(1)}, bf16[272,1024]{1,0:T(8,128)(2,1)}, u32[]{:S(2)}, u32[]{:S(2)}) collective-permute-start(bf16[272,1024]{1,0:T(8,128)(2,1)S(1)} %fusion.10.refs_0_.refs_4_), channel_id=1, source_target_pairs={{0,4},{1,5},{2,6},{3,7},{4,0},{5,1},{6,2},{7,3},{8,12},{9,13},{10,... | collective-permute-start | bytes 1671176 | tf_op jit(solution)/shard_map/ppermute | solution.py:389
  19.2 41.6 %collective-permute-start.2 = (bf16[272,1024]{1,0:T(8,128)(2,1)S(1)}, bf16[272,1024]{1,0:T(8,128)(2,1)}, u32[]{:S(2)}, u32[]{:S(2)}) collective-permute-start(bf16[272,1024]{1,0:T(8,128)(2,1)S(1)} %fusion.10.refs_0_.refs_4_), channel_id=1, source_target_pairs={{0,2},{1,3},{2,0},{3,1},{4,6},{5,7},{6,4},{7,5},{8,10},{9,11},{10,... | collective-permute-start | bytes 1671176 | tf_op jit(solution)/shard_map/ppermute | solution.py:389
  20.8 25.9 %collective-permute-start.10 = (bf16[64,896]{1,0:T(8,128)(2,1)}, bf16[64,896]{1,0:T(8,128)(2,1)S(1)}, u32[]{:S(2)}, u32[]{:S(2)}) collective-permute-start(bf16[64,896]{1,0:T(8,128)(2,1)} %get-tuple-element.114), channel_id=1, source_target_pairs={{0,6},{1,7},{2,4},{3,5},{4,2},{5,3},{6,0},{7,1},{8,14},{9,15},{10,... | collective-permute-start | bytes 344072 | tf_op jit(solution)/shard_map/ppermute | solution.py:389
  21.7 27.4 %collective-permute-start.32 = (bf16[64,896]{1,0:T(8,128)(2,1)}, bf16[64,896]{1,0:T(8,128)(2,1)S(1)}, u32[]{:S(2)}, u32[]{:S(2)}) collective-permute-start(bf16[64,896]{1,0:T(8,128)(2,1)} %get-tuple-element.115), channel_id=1, source_target_pairs={{0,2},{1,3},{2,0},{3,1},{4,6},{5,7},{6,4},{7,5},{8,10},{9,11},{10,... | collective-permute-start | bytes 344072 | tf_op jit(solution)/shard_map/ppermute | solution.py:389
  56.8 50.6 %collective-permute-start.42 = (bf16[160,1024]{1,0:T(8,128)(2,1)S(1)}, bf16[160,1024]{1,0:T(8,128)(2,1)}, u32[]{:S(2)}, u32[]{:S(2)}) collective-permute-start(bf16[160,1024]{1,0:T(8,128)(2,1)S(1)} %get-tuple-element.121.refs_22_), channel_id=1, source_target_pairs={{0,8},{1,9},{2,10},{3,11},{4,12},{5,13},{6,14},{7,15},{8,0},{9,1},... | collective-permute-start | bytes 983048 | tf_op jit(solution)/shard_map/ppermute | solution.py:389
  60.2 48.1 %collective-permute-start.22 = (bf16[160,1024]{1,0:T(8,128)(2,1)S(1)}, bf16[160,1024]{1,0:T(8,128)(2,1)S(1)}, u32[]{:S(2)}, u32[]{:S(2)}) collective-permute-start(bf16[160,1024]{1,0:T(8,128)(2,1)S(1)} %get-tuple-element.122.refs_18_.refs_17_), channel_id=1, source_target_pairs={{0,16},{16,0},{1,17},{17,1},{2,18},{18,2},{3,19},{19,3},{4,20},{20... | collective-permute-start | bytes 983048 | tf_op jit(solution)/shard_map/ppermute | solution.py:385
  66.5 41.5 %collective-permute-start.19 = (bf16[160,1024]{1,0:T(8,128)(2,1)S(1)}, bf16[160,1024]{1,0:T(8,128)(2,1)}, u32[]{:S(2)}, u32[]{:S(2)}) collective-permute-start(bf16[160,1024]{1,0:T(8,128)(2,1)S(1)} %get-tuple-element.122.refs_18_.refs_17_), channel_id=1, source_target_pairs={{0,8},{1,9},{2,10},{3,11},{4,12},{5,13},{6,14},{7,15},{8,0},{9,1},... | collective-permute-start | bytes 983048 | tf_op jit(solution)/shard_map/ppermute | solution.py:389
  67.0 53.8 %collective-permute-start.11 = (bf16[4,64,896]{2,1,0:T(8,128)(2,1)S(1)}, bf16[4,64,896]{2,1,0:T(8,128)(2,1)}, u32[]{:S(2)}, u32[]{:S(2)}) collective-permute-start(bf16[4,64,896]{2,1,0:T(8,128)(2,1)S(1)} %pad_maximum_fusion.refs_10_.refs_9_), channel_id=1, source_target_pairs={{0,8},{1,9},{2,10},{3,11},{4,12},{5,13},{6,14},{7,15},{8,0},{9,1},... | collective-permute-start | bytes 1376264 | tf_op jit(solution)/shard_map/ppermute | solution.py:389
  71.3 36.1 %collective-permute-start.5 = (bf16[4,2,448]{2,1,0:T(2,128)(2,1)S(1)}, bf16[4,2,448]{2,1,0:T(2,128)(2,1)S(1)}, u32[]{:S(2)}, u32[]{:S(2)}) collective-permute-start(bf16[4,2,448]{2,1,0:T(2,128)(2,1)S(1)} %pad_maximum_fusion.5), channel_id=1, source_target_pairs={{0,8},{1,9},{2,10},{3,11},{4,12},{5,13},{6,14},{7,15},{8,0},{9,1},... | collective-permute-start | bytes 21512 | tf_op jit(solution)/shard_map/ppermute | solution.py:389
  120.8 23.0 %collective-permute-start.35 = (bf16[4,64,896]{2,1,0:T(8,128)(2,1)S(1)}, bf16[4,64,896]{2,1,0:T(8,128)(2,1)}, u32[]{:S(2)}, u32[]{:S(2)}) collective-permute-start(bf16[4,64,896]{2,1,0:T(8,128)(2,1)S(1)} %pad_maximum_fusion.1.refs_14_), channel_id=1, source_target_pairs={{0,8},{1,9},{2,10},{3,11},{4,12},{5,13},{6,14},{7,15},{8,0},{9,1},... | collective-permute-start | bytes 1376264 | tf_op jit(solution)/shard_map/ppermute | solution.py:389
  120.8 23.0 %collective-permute-start.13 = (bf16[4,64,896]{2,1,0:T(8,128)(2,1)}, bf16[4,64,896]{2,1,0:T(8,128)(2,1)S(1)}, u32[]{:S(2)}, u32[]{:S(2)}) collective-permute-start(bf16[4,64,896]{2,1,0:T(8,128)(2,1)} %collective-permute-done.11.refs_11_.refs_10_), channel_id=1, source_target_pairs={{0,1},{1,0},{2,3},{3,2},{4,5},{5,4},{6,7},{7,6},{8,9},{9,8},{10,11... | collective-permute-start | bytes 1376264 | tf_op jit(solution)/shard_map/ppermute | solution.py:389
  121.3 18.9 %collective-permute-start.21 = (bf16[160,1024]{1,0:T(8,128)(2,1)}, bf16[160,1024]{1,0:T(8,128)(2,1)S(1)}, u32[]{:S(2)}, u32[]{:S(2)}) collective-permute-start(bf16[160,1024]{1,0:T(8,128)(2,1)} %collective-permute-done.19.refs_19_.refs_18_), channel_id=1, source_target_pairs={{0,1},{1,0},{2,3},{3,2},{4,5},{5,4},{6,7},{7,6},{8,9},{9,8},{10,11... | collective-permute-start | bytes 983048 | tf_op jit(solution)/shard_map/ppermute | solution.py:389
  124.3 20.2 %collective-permute-start.14 = (bf16[4,64,896]{2,1,0:T(8,128)(2,1)S(1)}, bf16[4,64,896]{2,1,0:T(8,128)(2,1)S(1)}, u32[]{:S(2)}, u32[]{:S(2)}) collective-permute-start(bf16[4,64,896]{2,1,0:T(8,128)(2,1)S(1)} %pad_maximum_fusion.refs_10_.refs_9_), channel_id=1, source_target_pairs={{0,16},{16,0},{1,17},{17,1},{2,18},{18,2},{3,19},{19,3},{4,20},{20... | collective-permute-start | bytes 1376264 | tf_op jit(solution)/shard_map/ppermute | solution.py:385
  124.4 20.7 %collective-permute-start.16 = (bf16[4,64,896]{2,1,0:T(8,128)(2,1)}, bf16[4,64,896]{2,1,0:T(8,128)(2,1)}, u32[]{:S(2)}, u32[]{:S(2)}) collective-permute-start(bf16[4,64,896]{2,1,0:T(8,128)(2,1)} %collective-permute-done.12.refs_12_.refs_11_), channel_id=1, source_target_pairs={{0,16},{16,0},{1,17},{17,1},{2,18},{18,2},{3,19},{19,3},{4,20},{20... | collective-permute-start | bytes 1376264 | tf_op jit(solution)/shard_map/ppermute | solution.py:385
  144.5 29.7 %collective-permute-start.36 = (bf16[4,64,896]{2,1,0:T(8,128)(2,1)S(1)}, bf16[4,64,896]{2,1,0:T(8,128)(2,1)}, u32[]{:S(2)}, u32[]{:S(2)}) collective-permute-start(bf16[4,64,896]{2,1,0:T(8,128)(2,1)S(1)} %pad_maximum_fusion.1.refs_14_), channel_id=1, source_target_pairs={{0,1},{1,0},{2,3},{3,2},{4,5},{5,4},{6,7},{7,6},{8,9},{9,8},{10,11... | collective-permute-start | bytes 1376264 | tf_op jit(solution)/shard_map/ppermute | solution.py:389
  145.0 29.1 %collective-permute-start.37 = (bf16[4,64,896]{2,1,0:T(8,128)(2,1)}, bf16[4,64,896]{2,1,0:T(8,128)(2,1)}, u32[]{:S(2)}, u32[]{:S(2)}) collective-permute-start(bf16[4,64,896]{2,1,0:T(8,128)(2,1)} %collective-permute-done.35.refs_15_), channel_id=1, source_target_pairs={{0,1},{1,0},{2,3},{3,2},{4,5},{5,4},{6,7},{7,6},{8,9},{9,8},{10,11... | collective-permute-start | bytes 1376264 | tf_op jit(solution)/shard_map/ppermute | solution.py:389
  148.7 25.2 %collective-permute-start.44 = (bf16[160,1024]{1,0:T(8,128)(2,1)}, bf16[160,1024]{1,0:T(8,128)(2,1)}, u32[]{:S(2)}, u32[]{:S(2)}) collective-permute-start(bf16[160,1024]{1,0:T(8,128)(2,1)} %collective-permute-done.42.refs_23_), channel_id=1, source_target_pairs={{0,1},{1,0},{2,3},{3,2},{4,5},{5,4},{6,7},{7,6},{8,9},{9,8},{10,11... | collective-permute-start | bytes 983048 | tf_op jit(solution)/shard_map/ppermute | solution.py:389
  241.9 59.2 %collective-permute-start.58 = (bf16[128,1024]{1,0:T(8,128)(2,1)S(1)}, bf16[128,1024]{1,0:T(8,128)(2,1)S(1)}, u32[]{:S(2)}, u32[]{:S(2)}) collective-permute-start(bf16[128,1024]{1,0:T(8,128)(2,1)S(1)} %copy-done.39), channel_id=1, source_target_pairs={{0,2},{1,3},{2,0},{3,1},{4,6},{5,7},{6,4},{7,5},{8,10},{9,11},{10,... | collective-permute-start | bytes 786440 | tf_op jit(solution)/shard_map/ppermute | solution.py:389
  242.3 65.3 %collective-permute-start.59 = (bf16[128,1024]{1,0:T(8,128)(2,1)}, bf16[128,1024]{1,0:T(8,128)(2,1)}, u32[]{:S(2)}, u32[]{:S(2)}) collective-permute-start(bf16[128,1024]{1,0:T(8,128)(2,1)} %get-tuple-element.79), channel_id=1, source_target_pairs={{0,4},{1,5},{2,6},{3,7},{4,0},{5,1},{6,2},{7,3},{8,12},{9,13},{10,... | collective-permute-start | bytes 786440 | tf_op jit(solution)/shard_map/ppermute | solution.py:389
  279.9 45.7 %collective-permute-start.83 = (bf16[4,160,1024]{2,1,0:T(8,128)(2,1)}, bf16[4,160,1024]{2,1,0:T(8,128)(2,1)}, u32[]{:S(2)}, u32[]{:S(2)}) collective-permute-start(bf16[4,160,1024]{2,1,0:T(8,128)(2,1)} %get-tuple-element.98), channel_id=1, source_target_pairs={{0,16},{16,0},{1,17},{17,1},{2,18},{18,2},{3,19},{19,3},{4,20},{20... | collective-permute-start | bytes 3932168 | tf_op jit(solution)/shard_map/ppermute | solution.py:385
  293.7 38.1 %collective-permute-start.70 = (bf16[4,4,64,896]{3,2,1,0:T(8,128)(2,1)}, bf16[4,4,64,896]{3,2,1,0:T(8,128)(2,1)S(1)}, u32[]{:S(2)}, u32[]{:S(2)}) collective-permute-start(bf16[4,4,64,896]{3,2,1,0:T(8,128)(2,1)} %get-tuple-element.92), channel_id=1, source_target_pairs={{0,16},{16,0},{1,17},{17,1},{2,18},{18,2},{3,19},{19,3},{4,20},{20... | collective-permute-start | bytes 5505032 | tf_op jit(solution)/shard_map/ppermute | solution.py:385
  301.0 27.1 %collective-permute-start.80 = (bf16[4,160,1024]{2,1,0:T(8,128)(2,1)}, bf16[4,160,1024]{2,1,0:T(8,128)(2,1)}, u32[]{:S(2)}, u32[]{:S(2)}) collective-permute-start(bf16[4,160,1024]{2,1,0:T(8,128)(2,1)} %get-tuple-element.95), channel_id=1, source_target_pairs={{0,16},{16,0},{1,17},{17,1},{2,18},{18,2},{3,19},{19,3},{4,20},{20... | collective-permute-start | bytes 3932168 | tf_op jit(solution)/shard_map/ppermute | solution.py:385
  307.4 26.2 %collective-permute-start.67 = (bf16[4,4,64,896]{3,2,1,0:T(8,128)(2,1)}, bf16[4,4,64,896]{3,2,1,0:T(8,128)(2,1)}, u32[]{:S(2)}, u32[]{:S(2)}) collective-permute-start(bf16[4,4,64,896]{3,2,1,0:T(8,128)(2,1)} %get-tuple-element.88), channel_id=1, source_target_pairs={{0,16},{16,0},{1,17},{17,1},{2,18},{18,2},{3,19},{19,3},{4,20},{20... | collective-permute-start | bytes 5505032 | tf_op jit(solution)/shard_map/ppermute | solution.py:385
  324.9 121.4 %collective-permute-start.61 = (f32[128,1024]{1,0:T(8,128)S(1)}, f32[128,1024]{1,0:T(8,128)S(1)}, u32[]{:S(2)}, u32[]{:S(2)}) collective-permute-start(f32[128,1024]{1,0:T(8,128)S(1)} %get-tuple-element.103), channel_id=1, source_target_pairs={{0,16},{16,0},{1,17},{17,1},{2,18},{18,2},{3,19},{19,3},{4,20},{20... | collective-permute-start | bytes 1572872 | tf_op jit(solution)/shard_map/ppermute | solution.py:385
  330.8 68.7 %collective-permute-start.81 = (bf16[2,160,1024]{2,1,0:T(8,128)(2,1)S(1)}, bf16[2,160,1024]{2,1,0:T(8,128)(2,1)S(1)}, u32[]{:S(2)}, u32[]{:S(2)}) collective-permute-start(bf16[2,160,1024]{2,1,0:T(8,128)(2,1)S(1)} %slice.359), channel_id=1, source_target_pairs={{0,1},{1,0},{2,3},{3,2},{4,5},{5,4},{6,7},{7,6},{8,9},{9,8},{10,11... | collective-permute-start | bytes 1966088 | tf_op jit(solution)/shard_map/ppermute | solution.py:389
  332.4 46.5 %collective-permute-start.71 = (bf16[2,4,64,896]{3,2,1,0:T(8,128)(2,1)S(1)}, bf16[2,4,64,896]{3,2,1,0:T(8,128)(2,1)S(1)}, u32[]{:S(2)}, u32[]{:S(2)}) collective-permute-start(bf16[2,4,64,896]{3,2,1,0:T(8,128)(2,1)S(1)} %slice.356), channel_id=1, source_target_pairs={{0,1},{1,0},{2,3},{3,2},{4,5},{5,4},{6,7},{7,6},{8,9},{9,8},{10,11... | collective-permute-start | bytes 2752520 | tf_op jit(solution)/shard_map/ppermute | solution.py:389
  335.8 62.3 %collective-permute-start.68 = (bf16[2,4,64,896]{3,2,1,0:T(8,128)(2,1)S(1)}, bf16[2,4,64,896]{3,2,1,0:T(8,128)(2,1)S(1)}, u32[]{:S(2)}, u32[]{:S(2)}) collective-permute-start(bf16[2,4,64,896]{3,2,1,0:T(8,128)(2,1)S(1)} %slice.357), channel_id=1, source_target_pairs={{0,1},{1,0},{2,3},{3,2},{4,5},{5,4},{6,7},{7,6},{8,9},{9,8},{10,11... | collective-permute-start | bytes 2752520 | tf_op jit(solution)/shard_map/ppermute | solution.py:389
  345.3 99.0 %collective-permute-start.85 = (bf16[160,1024]{1,0:T(8,128)(2,1)S(1)}, bf16[160,1024]{1,0:T(8,128)(2,1)S(1)}, u32[]{:S(2)}, u32[]{:S(2)}) collective-permute-start(bf16[160,1024]{1,0:T(8,128)(2,1)S(1)} %fusion.14), channel_id=1, source_target_pairs={{0,8},{1,9},{2,10},{3,11},{4,12},{5,13},{6,14},{7,15},{8,0},{9,1},... | collective-permute-start | bytes 983048 | tf_op jit(solution)/shard_map/ppermute | solution.py:389
  379.1 22.6 %collective-permute-start.72 = (bf16[4,64,896]{2,1,0:T(8,128)(2,1)S(1)}, bf16[4,64,896]{2,1,0:T(8,128)(2,1)S(1)}, u32[]{:S(2)}, u32[]{:S(2)}) collective-permute-start(bf16[4,64,896]{2,1,0:T(8,128)(2,1)S(1)} %fusion.12), channel_id=1, source_target_pairs={{0,8},{1,9},{2,10},{3,11},{4,12},{5,13},{6,14},{7,15},{8,0},{9,1},... | collective-permute-start | bytes 1376264 | tf_op jit(solution)/shard_map/ppermute | solution.py:389
  398.3 22.9 %collective-permute-start.69 = (bf16[4,64,896]{2,1,0:T(8,128)(2,1)S(1)}, bf16[4,64,896]{2,1,0:T(8,128)(2,1)S(1)}, u32[]{:S(2)}, u32[]{:S(2)}) collective-permute-start(bf16[4,64,896]{2,1,0:T(8,128)(2,1)S(1)} %fusion.11), channel_id=1, source_target_pairs={{0,8},{1,9},{2,10},{3,11},{4,12},{5,13},{6,14},{7,15},{8,0},{9,1},... | collective-permute-start | bytes 1376264 | tf_op jit(solution)/shard_map/ppermute | solution.py:389
  424.2 20.1 %collective-permute-start.82 = (bf16[160,1024]{1,0:T(8,128)(2,1)S(1)}, bf16[160,1024]{1,0:T(8,128)(2,1)S(1)}, u32[]{:S(2)}, u32[]{:S(2)}) collective-permute-start(bf16[160,1024]{1,0:T(8,128)(2,1)S(1)} %fusion.13), channel_id=1, source_target_pairs={{0,8},{1,9},{2,10},{3,11},{4,12},{5,13},{6,14},{7,15},{8,0},{9,1},... | collective-permute-start | bytes 983048 | tf_op jit(solution)/shard_map/ppermute | solution.py:389
  (102 other events, 1690.6 us)

commit v2 on v1

v2 whole, which is shorter than its diff:
```python
import functools

import jax
import jax.numpy as jnp
from jax import lax
from jax.experimental import pallas as pl
from jax.experimental.pallas import tpu as pltpu
from jax.sharding import PartitionSpec as P

D = 1024
PAIR = 128
FB = 512
CI = 3 * PAIR + FB
RO = PAIR + FB
EPS = 1e-05
NEG = -1000000000.0
SCALE = 0.125
ROWS = 128
TOK = 4 * ROWS
BF = jnp.bfloat16
F32 = jnp.float32
VMEM_LIMIT = 56 * 1024 * 1024


def mm(a, b):
    return lax.dot_general(a, b, (((1,), (0,)), ((), ())), preferred_element_type=F32)


def mm_nt(a, b):
    return lax.dot_general(a, b, (((1,), (1,)), ((), ())), preferred_element_type=F32)


def mm_tn(a, b):
    return lax.dot_general(a, b, (((0,), (0,)), ((), ())), preferred_element_type=F32)


def gelu(h):
    return 0.5 * h * (1.0 + jnp.tanh(0.7978845608 * (h + 0.044715 * h * h * h)))


def gelu_slope(h):
    th = jnp.tanh(0.7978845608 * (h + 0.044715 * h * h * h))
    inner = 0.7978845608 * (1.0 + 3 * 0.044715 * h * h)
    return 0.5 * (1.0 + th) + 0.5 * h * (1.0 - th * th) * inner


def partner(x):
    lane = lax.broadcasted_iota(jnp.int32, x.shape, 1)
    return jnp.where(lane % 2 == 0, pltpu.roll(x, PAIR - 1, 1), pltpu.roll(x, 1, 1))


def turned(x, cosine, sine):
    return x * cosine + partner(x) * sine


def by_head(x):
    lane = lax.broadcasted_iota(jnp.int32, (1, PAIR), 1)
    low = jnp.where(lane < 64, 1.0, 0.0).astype(x.dtype)
    high = jnp.where(lane < 64, 0.0, 1.0).astype(x.dtype)
    return jnp.concatenate([x * low, x * high], axis=0)


def beside(x):
    return jnp.concatenate([x[:ROWS], x[ROWS:]], axis=1)


def rows_of(j):
    return pl.ds(j * ROWS, ROWS)


def layer_norm_into(x_refs, gain_ref, bias_ref, normed):
    for j, x_ref in enumerate(x_refs):
        x = x_ref[0:ROWS, :].astype(F32)
        centered = x - jnp.mean(x, -1, keepdims=True)
        inv = lax.rsqrt(jnp.mean(centered * centered, -1, keepdims=True) + EPS)
        normed[rows_of(j), :] = (centered * inv * gain_ref[...] + bias_ref[...]).astype(BF)


def forward_in(g, normed, wi, bin_ref, cos_ref, sin_ref, mask_ref, qkv, probs, oa, pre):
    y = mm(normed[...], wi[g, :, 0 : 3 * PAIR])
    cosine, sine = cos_ref[...], sin_ref[...]
    qkv[g, :, 0:PAIR] = turned(y[:, 0:PAIR], cosine, sine).astype(BF)
    qkv[g, :, PAIR : 2 * PAIR] = turned(y[:, PAIR : 2 * PAIR], cosine, sine).astype(BF)
    qkv[g, :, 2 * PAIR : 3 * PAIR] = y[:, 2 * PAIR : 3 * PAIR].astype(BF)
    for j in range(4):
        q = qkv[g, rows_of(j), 0:PAIR]
        k = qkv[g, rows_of(j), PAIR : 2 * PAIR]
        v = qkv[g, rows_of(j), 2 * PAIR : 3 * PAIR]
        s = mm_nt(by_head(q), k) * SCALE
        allowed = mask_ref[j]
        s = jnp.where(jnp.concatenate([allowed, allowed], axis=0) > 0.5, s, NEG)
        e = jnp.exp(s - jnp.max(s, -1, keepdims=True))
        p = e / jnp.sum(e, -1, keepdims=True)
        probs[g, j] = p
        oa[g][rows_of(j), 0:PAIR] = mm(beside(p.astype(BF)), by_head(v)).astype(BF)
    h = mm(normed[...], wi[g, :, 3 * PAIR : CI]) + bin_ref[g : g + 1, :]
    pre[g] = h
    oa[g][:, PAIR:RO] = gelu(h).astype(BF)


def forward_out(oa, wo, outs):
    for n in range(4):
        cols = slice(n * 256, (n + 1) * 256)
        part = mm(oa[0][...], wo[0, :, cols]) + mm(oa[1][...], wo[1, :, cols])
        for j in range(4):
            outs[j][:, cols] = part[j * ROWS : (j + 1) * ROWS].astype(outs[j].dtype)


def backward_out(g, gout, wo, qkv, probs, pre, cos_ref, sin_ref, gcat, gbin_ref):
    go = mm_nt(gout[...], wo[g, 0:PAIR, :]).astype(BF)
    for j in range(4):
        q = qkv[g, rows_of(j), 0:PAIR]
        k = qkv[g, rows_of(j), PAIR : 2 * PAIR]
        v = qkv[g, rows_of(j), 2 * PAIR : 3 * PAIR]
        cosine, sine = cos_ref[rows_of(j), :], sin_ref[rows_of(j), :]
        go2 = by_head(go[j * ROWS : (j + 1) * ROWS])
        p = probs[g, j]
        gp = mm_nt(go2, v)
        gs = (p * (gp - jnp.sum(gp * p, -1, keepdims=True))).astype(BF)
        gv = mm_tn(p.astype(BF), go2)
        gq = mm(beside(gs), by_head(k)) * SCALE
        gk = mm_tn(gs, by_head(q)) * SCALE
        gcat[g][rows_of(j), 0:PAIR] = turned(gq, cosine, -sine).astype(BF)
        gcat[g][rows_of(j), PAIR : 2 * PAIR] = turned(gk, cosine, -sine).astype(BF)
        gcat[g][rows_of(j), 2 * PAIR : 3 * PAIR] = gv.astype(BF)
    ga = mm_nt(gout[...], wo[g, PAIR:RO, :])
    gpre = (ga * gelu_slope(pre[g])).astype(BF)
    gcat[g][:, 3 * PAIR : CI] = gpre
    gbin_ref[g : g + 1, :] = jnp.sum(gpre.astype(F32), 0, keepdims=True)


def backward_in(gcat, wi, outs):
    for n in range(4):
        cols = slice(n * 256, (n + 1) * 256)
        part = mm_nt(gcat[0][...], wi[0, cols, :]) + mm_nt(gcat[1][...], wi[1, cols, :])
        for j in range(4):
            outs[j][:, cols] = part[j * ROWS : (j + 1) * ROWS].astype(outs[j].dtype)


A_COLS = D + 2 * RO
B_COLS = CI + 512


def views_a(ship_a):
    return ship_a.at[:, 0:D], (ship_a.at[:, D : D + RO], ship_a.at[:, D + RO : D + 2 * RO])


def views_b(ship_b):
    return ship_b.at[:, 0:CI], ship_b.at[:, CI : CI + 512]


def input_copies(fast, refs, wi, sems):
    if not fast:
        return [pltpu.make_async_copy(refs[0], wi, sems.at[0])]
    return [pltpu.make_async_copy(refs[slot], wi.at[slot], sems.at[slot]) for slot in range(2)]


def output_copies(fast, refs, wo, sems):
    if not fast:
        return [pltpu.make_async_copy(refs[0], wo, sems.at[0])]
    core = lax.axis_index("section")
    copies = []
    for own in range(2):
        half = core if own == 0 else 1 - core
        cols = pl.ds(pl.multiple_of(512 * half, 512), 512)
        for g in range(2):
            slot = jnp.bitwise_xor(core, g)
            copies.append(
                pltpu.make_async_copy(refs[own].at[g], wo.at[slot, :, cols], sems.at[len(copies)])
            )
    return copies


def place_of():
    return lax.axis_index("dp"), lax.axis_index("section")


def other_half(fast, gout, half_ref):
    core = lax.axis_index("section") if fast else 0
    half_ref[...] = gout[:, pl.ds(pl.multiple_of(512 * (1 - core), 512), 512)]


def join_in_kernel(*refs):
    near_own, near_far_a, near_far_b, own, far_a, far_b = refs[:6]
    joined, sems = refs[6:]
    me, _ = place_of()
    copies = []
    for flip, pieces in ((0, own), (8, (far_a, far_b)), (1, near_own), (9, (near_far_a, near_far_b))):
        for j in range(4):
            piece = pieces[j // 2].at[j % 2] if isinstance(pieces, tuple) else pieces.at[j]
            start = pl.multiple_of(jnp.bitwise_xor(me, flip ^ (2 * j)) * 64, 64)
            copies.append(pltpu.make_async_copy(piece, joined.at[pl.ds(start, 64), :], sems.at[len(copies)]))
            copies[-1].start()
    for copy in copies:
        copy.wait()


def join_out_kernel(own, far, near_own, near_far, joined, sems):
    me, _ = place_of()
    copies = []
    for flip, piece in ((0, own), (8, far), (1, near_own), (9, near_far)):
        source = jnp.bitwise_xor(me, flip)
        g, r = source // 8, source % 2
        first, second = pl.multiple_of(64 * r, 64), pl.multiple_of(PAIR + 256 * r, 128)
        for rows, target in ((slice(0, 64), pl.ds(first, 64)), (slice(64, 320), pl.ds(second, 256))):
            copies.append(pltpu.make_async_copy(piece.at[rows], joined.at[g, target], sems.at[len(copies)]))
            copies[-1].start()
    for copy in copies:
        copy.wait()


def first_forward_kernel(fast, n, *refs):
    x_refs, refs = refs[:4], refs[4:]
    (gain, bias, bin_ref, cos_ref, sin_ref, mask_ref), refs = refs[:6], refs[6:]
    wi_refs, wo_refs, refs = refs[:n], refs[n : 2 * n], refs[2 * n :]
    outs, refs = refs[:4], refs[4:]
    ship_a, qkv, probs, pre, wi, wo, sem_i, sem_o = refs
    normed, oa = views_a(ship_a)
    loads_i, loads_o = input_copies(fast, wi_refs, wi, sem_i), output_copies(fast, wo_refs, wo, sem_o)
    for copy in loads_i + loads_o:
        copy.start()
    layer_norm_into(x_refs, gain, bias, normed)
    for copy in loads_i:
        copy.wait()
    for g in range(2):
        forward_in(g, normed, wi, bin_ref, cos_ref, sin_ref, mask_ref, qkv, probs, oa, pre)
    for copy in loads_o:
        copy.wait()
    forward_out(oa, wo, outs)


def second_layer_kernel(fast, n, *refs):
    x_refs, gout_refs, refs = refs[:4], refs[4:8], refs[8:]
    (gain, bias, bin_ref, cos_ref, sin_ref, mask_ref), refs = refs[:6], refs[6:]
    wi_refs, wo_refs, refs = refs[:n], refs[n : 2 * n], refs[2 * n :]
    outs, gouts, refs = refs[:4], refs[4:8], refs[8:]
    ship_a, ship_b, gcat0, gbin_ref, qkv, probs, pre, gout, wi, wo, sem_i, sem_o = refs
    normed, oa = views_a(ship_a)
    gcat1, gout_half = views_b(ship_b)
    gcat = (gcat0, gcat1)
    loads_i, loads_o = input_copies(fast, wi_refs, wi, sem_i), output_copies(fast, wo_refs, wo, sem_o)
    for copy in loads_i + loads_o:
        copy.start()
    layer_norm_into(x_refs, gain, bias, normed)
    for j in range(4):
        gout[rows_of(j), :] = gout_refs[j][...]
    other_half(fast, gout, gout_half)
    for copy in loads_i:
        copy.wait()
    for g in range(2):
        forward_in(g, normed, wi, bin_ref, cos_ref, sin_ref, mask_ref, qkv, probs, oa, pre)
    for copy in loads_o:
        copy.wait()
    for g in range(2):
        backward_out(g, gout, wo, qkv, probs, pre, cos_ref, sin_ref, gcat, gbin_ref)
    backward_in(gcat, wi, gouts)
    forward_out(oa, wo, outs)


def first_backward_kernel(fast, n, *refs):
    gout_refs, refs = refs[:4], refs[4:]
    (cos_ref, sin_ref, qkv, probs, pre), refs = refs[:5], refs[5:]
    wi_refs, wo_refs, refs = refs[:n], refs[n : 2 * n], refs[2 * n :]
    gouts, refs = refs[:4], refs[4:]
    ship_b, gcat0, gbin_ref, gout, wi, wo, sem_i, sem_o = refs
    gcat1, gout_half = views_b(ship_b)
    gcat = (gcat0, gcat1)
    loads_i, loads_o = input_copies(fast, wi_refs, wi, sem_i), output_copies(fast, wo_refs, wo, sem_o)
    for copy in loads_o + loads_i:
        copy.start()
    for j in range(4):
        gout[rows_of(j), :] = gout_refs[j][...]
    other_half(fast, gout, gout_half)
    for copy in loads_o:
        copy.wait()
    for g in range(2):
        backward_out(g, gout, wo, qkv, probs, pre, cos_ref, sin_ref, gcat, gbin_ref)
    for copy in loads_i:
        copy.wait()
    backward_in(gcat, wi, gouts)


def weight_grad_out_kernel(*refs):
    gout_refs, (ship_a, other_a, other_b, keep, send, left, right) = refs[:4], refs[4:]
    me, core = place_of()
    cols = pl.ds(pl.multiple_of(512 * core, 512), 512)
    for j in range(4):
        right[rows_of(j), :] = gout_refs[j][:, cols]
    right[TOK : 2 * TOK, :] = other_b[:, CI : CI + 512]
    for side, ship in enumerate((ship_a, other_a)):
        tokens = slice(side * TOK, (side + 1) * TOK)
        for part in range(2):
            far = jnp.bitwise_xor(me // 8, jnp.bitwise_xor(core, part ^ side))
            flat = ship[:, D + part * RO : D + (part + 1) * RO].T
            for r in range(2):
                near = jnp.bitwise_xor(me % 2, r)
                left[near, far, 0:64, tokens] = flat[64 * r : 64 * r + 64]
                left[near, far, 64:320, tokens] = flat[PAIR + 256 * r : PAIR + 256 * (r + 1)]
    for near, out in ((1, send), (0, keep)):
        for far in range(2):
            out[far] = mm(left[near, far], right[...]).astype(BF)


def weight_grad_in_kernel(ship_a, other_a, gcat, other_b, keep_a, keep_b, send_a, send_b, left, right):
    me, _ = place_of()
    g, t, r = me // 8, (me // 2) % 4, me % 2
    right[0:TOK, :] = gcat[...]
    right[TOK : 2 * TOK, :] = other_b[:, 0:CI]
    for side, ship in enumerate((ship_a, other_a)):
        tokens = slice(side * TOK, (side + 1) * TOK)
        for far in range(2):
            for j in range(4):
                pair = jnp.bitwise_xor(g, far) * 4 + jnp.bitwise_xor(t, j)
                block = ship[:, pl.ds(pl.multiple_of(pair * PAIR, PAIR), PAIR)].T
                for s in range(2):
                    near = jnp.bitwise_xor(r, s)
                    start = (far * 2 + j % 2) * 64
                    left[near, j // 2, start : start + 64, tokens] = block[64 * s : 64 * s + 64]
    for near, half, out in ((1, 0, send_a), (1, 1, send_b), (0, 0, keep_a), (0, 1, keep_b)):
        part = mm(left[near, half], right[...]).astype(BF)
        for i in range(4):
            out[i // 2, i % 2] = part[64 * i : 64 * i + 64]


def whole_grad_out_kernel(*refs):
    gout_refs, (ship_a, out, gout) = refs[:4], refs[4:]
    for j in range(4):
        gout[rows_of(j), :] = gout_refs[j][...]
    for g in range(2):
        out[g] = mm_tn(ship_a[:, D + g * RO : D + (g + 1) * RO], gout[...]).astype(BF)


def whole_grad_in_kernel(ship_a, gcat0, ship_b, out):
    for g in range(2):
        right = gcat0[...] if g == 0 else ship_b[:, 0:CI]
        for m in range(4):
            rows = slice(m * 256, (m + 1) * 256)
            out[g, rows, :] = mm_tn(ship_a[:, rows], right).astype(BF)


def norm_backward_kernel(own, r1, r2, r3, x_ref, gout_ref, gain, gx_ref, low_ref, sums_ref):
    x = x_ref[0:ROWS, :].astype(F32)
    gn = own[...] + r1[...].astype(F32) + r2[...].astype(F32) + r3[...].astype(F32)
    gout = gout_ref[...].astype(F32)
    centered = x - jnp.mean(x, -1, keepdims=True)
    inv = lax.rsqrt(jnp.mean(centered * centered, -1, keepdims=True) + EPS)
    unit = centered * inv
    gu = gn * gain[...]
    gx = gout + inv * (gu - jnp.mean(gu, -1, keepdims=True) - unit * jnp.mean(gu * unit, -1, keepdims=True))
    gx_ref[...] = gx
    low_ref[...] = gx.astype(BF)
    sums_ref[0:1, :] = jnp.sum(gn * unit, 0, keepdims=True)
    sums_ref[1:2, :] = jnp.sum(gn, 0, keepdims=True)
    sums_ref[2:3, :] = jnp.sum(gout, 0, keepdims=True)


def pack_kernel(w_qkv, w_out, w_in, w_fc, wi_keep, wi_send, wo_keep, wo_send):
    t, core = (lax.axis_index("dp") // 2) % 4, lax.axis_index("section")
    for ref, g in ((wi_keep, core), (wi_send, 1 - core)):
        for j in range(4):
            rank = jnp.bitwise_xor(t, j)
            for part in range(3):
                start = pl.multiple_of(part * D + g * 512 + rank * PAIR, PAIR)
                ref[j, :, part * PAIR : (part + 1) * PAIR] = w_qkv[:, pl.ds(start, PAIR)].astype(BF)
            start = pl.multiple_of(g * 2048 + rank * FB, FB)
            ref[j, :, 3 * PAIR : CI] = w_in[:, pl.ds(start, FB)].astype(BF)
    for ref, half in ((wo_keep, core), (wo_send, 1 - core)):
        cols = pl.ds(pl.multiple_of(512 * half, 512), 512)
        ref[0:64, :] = w_out[:, cols].astype(BF)
        ref[64:320, :] = w_fc[:, cols].astype(BF)


def unpack_kernel(own0, own1, own2, own3, other, wo_own, wo_other, g_qkv, g_out, g_in, g_fc):
    t, core = (lax.axis_index("dp") // 2) % 4, lax.axis_index("section")
    for side, g in ((0, core), (1, 1 - core)):
        for j in range(4):
            block = (own0, own1, own2, own3)[j][...] if side == 0 else other[j]
            block = block.astype(F32)
            rank = jnp.bitwise_xor(t, j)
            for part in range(3):
                start = pl.multiple_of(part * D + g * 512 + rank * PAIR, PAIR)
                g_qkv[:, pl.ds(start, PAIR)] = block[:, part * PAIR : (part + 1) * PAIR]
            start = pl.multiple_of(g * 2048 + rank * FB, FB)
            g_in[:, pl.ds(start, FB)] = block[:, 3 * PAIR : CI]
    for ref, half in ((wo_own, core), (wo_other, 1 - core)):
        cols = pl.ds(pl.multiple_of(512 * half, 512), 512)
        g_out[:, cols] = ref[0:64, :].astype(F32)
        g_fc[:, cols] = ref[64:320, :].astype(F32)


VM = pl.BlockSpec(memory_space=pltpu.VMEM)
HB = pl.BlockSpec(memory_space=pl.ANY)


def kernel_call(kernel, args, outs, any_args=0, any_outs=False, scratch=(), flops=1e6, name=None):
    sizes = [a.size * a.dtype.itemsize for a in args] + [a.size * a.dtype.itemsize for a in outs]
    return pl.pallas_call(
        kernel,
        out_shape=outs,
        in_specs=[VM] * (len(args) - any_args) + [HB] * any_args,
        out_specs=[HB if any_outs else VM] * len(outs),
        scratch_shapes=list(scratch),
        compiler_params=pltpu.CompilerParams(vmem_limit_bytes=VMEM_LIMIT),
        cost_estimate=pl.CostEstimate(flops=int(flops), bytes_accessed=int(sum(sizes)), transcendentals=0),
        name=name,
    )(*args)


def arr(shape, dtype):
    return jax.ShapeDtypeStruct(shape, dtype)


def weight_scratch(fast):
    return [
        pltpu.VMEM((2, D, CI), BF),
        pltpu.VMEM((2, RO, D), BF),
        pltpu.SemaphoreType.DMA((2 if fast else 1,)),
        pltpu.SemaphoreType.DMA((4 if fast else 1,)),
    ]


def partial_outs():
    return [arr((ROWS, D), F32)] + [arr((ROWS, D), BF)] * 3


def swap_core(value):
    return lax.ppermute(value, "section", [(0, 1), (1, 0)])


def flipped(value, flip):
    count = lax.axis_size("dp")
    return lax.ppermute(value, "dp", [(i, i ^ flip) for i in range(count)])


def after(value, *earlier):
    return lax.optimization_barrier((value, earlier))[0]


def choose(own, other):
    first_core = lax.axis_index("section") == 0
    return jnp.where(first_core, own, other), jnp.where(first_core, other, own)


def across(values):
    spread = lax.axis_size("dp") // 8
    return [flipped(v, (j + 1) * spread) for j, v in enumerate(values)]


def groups_of(spread):
    places = [[[g * 4 * spread + t * spread + r for r in range(spread)] for t in range(4)] for g in range(2)]
    t_groups = [[places[g][t][r] for t in range(4)] for g in range(2) for r in range(spread)]
    f_groups = [[places[g][t][r] for g in range(2) for r in range(spread)] for t in range(4)]
    return t_groups, f_groups


def any_gather(w_qkv, w_out, w_in, w_fc):
    share, spread = w_qkv.shape[0], lax.axis_size("dp") // 8
    t_groups, f_groups = groups_of(spread)
    qkv = w_qkv.reshape(share, 3, 2, 4, PAIR).transpose(3, 0, 2, 1, 4).reshape(4, share, 2, 3 * PAIR)
    wi = jnp.concatenate([qkv, w_in.reshape(share, 2, 4, FB).transpose(2, 0, 1, 3)], axis=-1).astype(BF)
    wi = lax.all_to_all(wi, "dp", 0, 0, axis_index_groups=t_groups, tiled=True)
    wi = lax.all_gather(wi, "dp", axis_index_groups=f_groups)
    wi = wi.reshape(2, spread, 4, share, 2, CI).transpose(4, 0, 2, 1, 3, 5).reshape(2, D, CI)
    wo = lax.all_gather(w_out.astype(BF), "dp", axis_index_groups=f_groups).reshape(2, PAIR, D)
    wf = lax.all_gather(w_fc.astype(BF), "dp", axis_index_groups=f_groups).reshape(2, FB, D)
    wo = jnp.concatenate([wo, wf], axis=1)
    return choose(wi, swap_core(wi)), choose(wo, swap_core(wo))


def any_reduce(gi, go):
    count = lax.axis_size("dp")
    spread, share = count // 8, D // count
    t_groups, f_groups = groups_of(spread)

    def scattered(value):
        return lax.psum_scatter(value, "dp", scatter_dimension=0, axis_index_groups=f_groups)

    gi = gi.reshape(2, 2, 4, spread, share, CI).transpose(1, 3, 2, 4, 0, 5).reshape(2 * spread, 4, share, 2, CI)
    gi = lax.all_to_all(scattered(gi), "dp", 0, 0, axis_index_groups=t_groups, tiled=True)
    g_qkv = gi[..., : 3 * PAIR].reshape(4, share, 2, 3, PAIR).transpose(1, 3, 2, 0, 4).reshape(share, 3 * D)
    g_in = gi[..., 3 * PAIR :].transpose(1, 2, 0, 3).reshape(share, 4 * D)
    g_out = scattered(go[:, :PAIR].reshape(2 * spread, share, D))
    g_fc = scattered(go[:, PAIR:].reshape(2 * spread, 4 * share, D))
    return g_qkv, g_out, g_in, g_fc


def body(boundary, segments, ln_gain, ln_bias, w_qkv, w_out, w_in, b_in, w_fc, b_fc):
    core, me = lax.axis_index("section"), lax.axis_index("dp")
    count = lax.axis_size("dp")
    fast = count == 16
    spread = count // 8
    rank = (me // spread) % 4
    share = D // count
    width_small = 7 * share
    first_core = core == 0

    if fast:
        wi_keep, wi_send, wo_keep, wo_send = kernel_call(
            pack_kernel,
            [w_qkv[0], w_out[0], w_in[0], w_fc[0]],
            [arr((4, 64, CI), BF), arr((4, 64, CI), BF), arr((320, 512), BF), arr((320, 512), BF)],
            name="pack",
        )
        wi_recv, wo_recv = swap_core(wi_send), swap_core(wo_send)
        wi_first = [choose(wi_keep[j], wi_recv[j]) for j in range(4)]
        wo_first = choose(wo_keep, wo_recv)
        boundary, ln_gain = after((boundary, ln_gain), wi_keep)
    else:
        wi_both, wo_both = any_gather(w_qkv[0], w_out[0], w_in[0], w_fc[0])

    swapped = swap_core(lax.dynamic_index_in_dim(boundary[0], 1 - core, 0, False)[0])
    kept = lax.dynamic_index_in_dim(boundary[0], core, 0, False)[0]
    x0, g1 = choose(kept, swapped)
    small = jnp.concatenate([ln_gain, ln_bias, b_fc, b_in], axis=-1).astype(BF)
    small = jnp.concatenate(choose(small, swap_core(small)))
    seg = lax.dynamic_index_in_dim(segments, core, 0, False)[0].astype(BF)
    extra = jnp.zeros((16, D), BF).at[0, :ROWS].set(seg)
    if fast:
        extra = extra.at[1:3, :width_small].set(small)
    pack = jnp.concatenate([x0, extra])

    if fast:

        def join(wi_pieces, wo_pieces, name):
            wo = kernel_call(
                join_out_kernel,
                wo_pieces,
                [arr((2, RO, 512), BF)],
                any_args=4,
                any_outs=True,
                scratch=[pltpu.SemaphoreType.DMA((8,))],
                name=name + "_out",
            )[0]
            wi = kernel_call(
                join_in_kernel,
                wi_pieces,
                [arr((D, CI), BF)],
                any_args=6,
                any_outs=True,
                scratch=[pltpu.SemaphoreType.DMA((16,))],
                name=name + "_in",
            )[0]
            return [wi, swap_core(wi)], [wo, swap_core(wo)]

        mine = [w[0] for w in wi_first]
        arrived = across(mine[1:])
        wo_own = wo_first[0]
        wo_far = flipped(wo_own, 8)
        wo_near = flipped(wo_own, 1)
        wi_own = jnp.stack([mine[0]] + arrived)
        a_far = flipped(wi_own[0:2], 8)
        wi_near = flipped(wi_own, 1)
        b_far = flipped(after(wi_own[2:4], a_far), 8)
        wo_near_far = flipped(after(wo_far, wo_near), 1)
        a_near = flipped(after(a_far, wi_near), 1)
        b_near = flipped(b_far, 1)
        wi0, wo0 = join([wi_near, a_near, b_near, wi_own, a_far, b_far], [wo_own, wo_far, wo_near, wo_near_far], "join0")
        packs = [pack] + across(after([pack] * 3, arrived))
        mine = [w[1] for w in wi_first]
        arrived = across(after(mine[1:], packs[1:]))
        wo_own = wo_first[1]
        wi_own = jnp.stack([mine[0]] + arrived)
        wo_far, a_far = flipped(after(wo_own, b_far), 8), flipped(after(wi_own[0:2], b_far), 8)
        wo_near = flipped(after(wo_own, b_near), 1)
        wi_near = flipped(after(wi_own, b_near), 1)
        b_far = flipped(after(wi_own[2:4], wo_far), 8)
        wo_near_far = flipped(after(wo_far, wo_near), 1)
        a_near = flipped(after(a_far, wi_near), 1)
        b_near = flipped(b_far, 1)
        wi1, wo1 = join([wi_near, a_near, b_near, wi_own, a_far, b_far], [wo_own, wo_far, wo_near, wo_near_far], "join1")
        g1s = [g1] + across(after([g1] * 3, wi0[0]))

        held = jnp.stack([p[129:131, :width_small] for p in packs])
        held = jnp.concatenate([held, flipped(held, 8)])
        held = jnp.concatenate([held, flipped(held, 1)]).reshape(16, 2 * width_small)
        index = jnp.arange(16)
        flip_of = jnp.bitwise_xor(index, me)
        at = (flip_of % 2) * 8 + (flip_of // 8) * 4 + (flip_of // 2) % 4
        onehot = (at[:, None] == index[None, :]).astype(BF)
        everyone = mm(onehot, held).reshape(16, 2, width_small)
    else:
        wi0, wi1 = [wi_both[0]], [wi_both[1]]
        wo0, wo1 = [wo_both[0]], [wo_both[1]]
        packs, g1s = [pack] + across([pack] * 3), [g1] + across([g1] * 3)
        everyone = lax.all_gather(small, "dp").astype(F32)
    n = len(wi0)

    def parts_in_place(value):
        return jnp.where(first_core, value, value[::-1]) if fast else value

    def small_of(layer):
        one = everyone[:, layer]
        vectors = [one[:, i * share : (i + 1) * share].reshape(1, D) for i in range(3)]
        b = one[:, 3 * share :].reshape(2, 4, FB)
        return *vectors, parts_in_place(lax.dynamic_index_in_dim(b, rank, 1, False))

    gain0, bias0, bfc0, bin0 = small_of(0)
    gain1, bias1, bfc1, bin1 = small_of(1)

    segs = jnp.stack([p[ROWS, :ROWS] for p in packs])
    row = lax.broadcasted_iota(jnp.int32, (ROWS, ROWS), 0)
    col = lax.broadcasted_iota(jnp.int32, (ROWS, ROWS), 1)
    mask = ((segs[:, :, None] == segs[:, None, :]) & (col <= row)).astype(F32)
    positions = jnp.sum(mask, -1).reshape(TOK, 1) - 1.0
    lane = jnp.arange(PAIR) % 64
    freq = jnp.where(lane < 32, 10000.0 ** (-(lane // 2 * 2).astype(F32) / 32), 0.0)
    angle = positions * freq
    cosine = jnp.cos(angle)
    sine = jnp.sin(angle) * jnp.where(lane % 2 == 0, -1.0, 1.0)

    layer_flops = 2 * TOK * 2 * (D * CI + RO * D)
    saved = [
        arr((TOK, A_COLS), BF),
        arr((2, TOK, 3 * PAIR), BF),
        arr((2, 4, 2 * ROWS, ROWS), F32),
        arr((2, TOK, FB), F32),
    ]
    got = kernel_call(
        functools.partial(first_forward_kernel, fast, n),
        [*packs, gain0, bias0, bin0, cosine, sine, mask, *wi0, *wo0],
        partial_outs() + saved,
        any_args=2 * n,
        scratch=weight_scratch(fast),
        flops=layer_flops,
        name="first_forward",
    )
    own, sends, (ship_a0, qkv0, probs0, pre0) = got[0], got[1:4], got[4:]

    def total(own, sends):
        return sum([r.astype(F32) for r in across(sends)], own)

    x1 = (x0.astype(F32) + total(own, sends) + bfc0).astype(BF)
    x1s = [x1] + across([x1] * 3)

    back_outs = [arr((TOK, B_COLS), BF), arr((TOK, CI), BF), arr((2, FB), F32)]
    got = kernel_call(
        functools.partial(second_layer_kernel, fast, n),
        [*x1s, *g1s, gain1, bias1, bin1, cosine, sine, mask, *wi1, *wo1],
        partial_outs()
        + partial_outs()
        + [arr((TOK, A_COLS), BF)]
        + back_outs,
        any_args=2 * n,
        scratch=[
            pltpu.VMEM((2, TOK, 3 * PAIR), BF),
            pltpu.VMEM((2, 4, 2 * ROWS, ROWS), F32),
            pltpu.VMEM((2, TOK, FB), F32),
            pltpu.VMEM((TOK, D), BF),
        ]
        + weight_scratch(fast),
        flops=2 * layer_flops,
        name="second_layer",
    )
    out_own, out_sends, gn_own, gn_sends = got[0], got[1:4], got[4], got[5:8]
    ship_a1, ship_b1, gcat1, gbin1 = got[8:]

    def norm_backward(own, arrived, x, gout, gain, name):
        return kernel_call(
            norm_backward_kernel,
            [own, *arrived, x, gout, gain],
            [arr((ROWS, D), F32), arr((ROWS, D), BF), arr((3, D), F32)],
            name=name,
        )

    def weight_grads(gouts, ship_a, ship_b, gcat, name):
        grad_flops = 2 * TOK * 2 * (CI + RO) * D // 2
        if fast:
            other_a, other_b = swap_core(ship_a), swap_core(ship_b)
            go = kernel_call(
                weight_grad_out_kernel,
                [*gouts, ship_a, other_a, other_b],
                [arr((2, 320, 512), BF)] * 2,
                scratch=[pltpu.VMEM((2, 2, 320, 2 * TOK), BF), pltpu.VMEM((2 * TOK, 512), BF)],
                flops=grad_flops,
                name=name + "_out",
            )
            gi = kernel_call(
                weight_grad_in_kernel,
                [ship_a, other_a, gcat, other_b],
                [arr((2, 2, 64, CI), BF)] * 4,
                scratch=[pltpu.VMEM((2, 2, 256, 2 * TOK), BF), pltpu.VMEM((2 * TOK, CI), BF)],
                flops=grad_flops,
                name=name + "_in",
            )
            return go, gi
        go = kernel_call(
            whole_grad_out_kernel,
            [*gouts, ship_a],
            [arr((2, RO, D), BF)],
            scratch=[pltpu.VMEM((TOK, D), BF)],
            flops=grad_flops,
            name=name + "_out",
        )
        gi = kernel_call(
            whole_grad_in_kernel, [ship_a, gcat, ship_b], [arr((2, D, CI), BF)], flops=grad_flops, name=name + "_in"
        )
        return go, gi

    grads1 = weight_grads(g1s, ship_a1, ship_b1, gcat1, "grads1")
    _, g0, sums1 = norm_backward(after(gn_own, grads1), across(gn_sends), x1, g1, gain1, "norm_backward1")
    g0s = [g0] + across([g0] * 3)
    out1 = x1.astype(F32) + total(out_own, after(out_sends, g0s[1:])) + bfc1

    got = kernel_call(
        functools.partial(first_backward_kernel, fast, n),
        [*g0s, cosine, sine, qkv0, probs0, pre0, *wi0, *wo0],
        partial_outs() + back_outs,
        any_args=2 * n,
        scratch=[pltpu.VMEM((TOK, D), BF)] + weight_scratch(fast),
        flops=layer_flops,
        name="first_backward",
    )
    gn_own, gn_sends, (ship_b0, gcat0, gbin0) = got[0], got[1:4], got[4:]
    grads0 = weight_grads(g0s, ship_a0, ship_b0, gcat0, "grads0")
    gx0, _, sums0 = norm_backward(gn_own, across(gn_sends), x0, g0, gain0, "norm_backward0")

    arrived = swap_core(jnp.where(first_core, out1, gx0))
    boundary_out = jnp.where(first_core, jnp.stack([gx0, arrived]), jnp.stack([arrived, out1]))[None, :, None]

    def small_grads(sums, gbin):
        vectors = sums.reshape(3, count, share).transpose(1, 0, 2).reshape(count, 3 * share)
        onehot = (jnp.arange(4) == rank).astype(F32)
        b = parts_in_place(gbin).reshape(2, 1, spread, 4 * share) * onehot[None, :, None, None]
        return jnp.concatenate([vectors, b.reshape(count, 4 * share)], axis=1)

    both = choose(small_grads(sums0, gbin0), small_grads(sums1, gbin1))
    vector = both[0] + swap_core(both[1])
    if fast:
        for flip in (2, 4, 1, 8):
            vector = vector + flipped(vector, flip)
        vector = lax.dynamic_index_in_dim(vector, me, 0, True)
    else:
        vector = lax.psum_scatter(vector, "dp", scatter_dimension=0, tiled=True)
    g_gain, g_bias, g_bfc = (vector[:, i * share : (i + 1) * share] for i in range(3))
    g_bin = vector[:, 3 * share :]

    if fast:

        def reduce_over_f(keep, send):
            near = flipped(send, 1)
            onward = flipped((keep[1].astype(F32) + near[1].astype(F32)).astype(BF), 8)
            return (keep[0].astype(F32) + near[0].astype(F32) + onward.astype(F32)).astype(BF)

        def reduced(grads):
            (wo_keep, wo_send), (keep_a, keep_b, send_a, send_b) = grads
            wo = reduce_over_f(wo_keep, wo_send)
            a, b = reduce_over_f(keep_a, send_a), reduce_over_f(keep_b, send_b)
            return wo, [a[0]] + across([a[1], b[0], b[1]])

        (wo_1, wi_1), (wo_0, wi_0) = reduced(grads1), reduced(grads0)
        wo_mine, wo_theirs = choose(wo_0, wo_1)
        pairs = [choose(a, b) for a, b in zip(wi_0, wi_1)]
        wi_other = swap_core(jnp.stack([p[1] for p in pairs]))
        g_qkv, g_out, g_in, g_fc = kernel_call(
            unpack_kernel,
            [*[p[0] for p in pairs], wi_other, wo_mine, swap_core(wo_theirs)],
            [arr((64, 3 * D), F32), arr((64, D), F32), arr((64, 4 * D), F32), arr((256, D), F32)],
            name="unpack",
        )
    else:
        (go1,), (gi1,) = grads1
        (go0,), (gi0,) = grads0
        mine, theirs = choose(gi0, gi1)
        gi = mine.astype(F32) + swap_core(theirs).astype(F32)
        mine, theirs = choose(go0, go1)
        go = mine.astype(F32) + swap_core(theirs).astype(F32)
        g_qkv, g_out, g_in, g_fc = any_reduce(gi, go)

    return (boundary_out, g_gain, g_bias, g_qkv[None], g_out[None], g_in[None], g_bin, g_fc[None], g_bfc)


def solution(mesh):
    rows = P("section", None, "dp", None, None)
    vector, matrix = P("section", "dp"), P("section", "dp", None)
    return jax.shard_map(
        body,
        mesh=mesh,
        in_specs=(rows, P(None, "dp", None), vector, vector, matrix, matrix, matrix, vector, matrix, vector),
        out_specs=(rows, vector, vector, matrix, matrix, matrix, vector, matrix, vector),
        check_vma=False,
    )
```

time: 456 us -> 608 us (1.33)
  Pallas kernels: 82.9 us -> 279 us
  waiting for transfers between devices: 254 us -> 178 us
  starting transfers between devices: 70.3 us -> 104 us
    pallas_call x11 -> x15, Pallas kernels: 82.9 us -> 279 us  [kernel_call(): pl.pallas_call(kernel, out_shape=outs, in_specs=[VM] * (len(args) - any_a...]
    ppermute x59 -> x70, waiting for transfers between devices: 252 us -> 174 us  [flipped(): return lax.ppermute(value, 'dp', [(i, i ^ flip) for i in range(count)])]
    ppermute x59 -> x70, starting transfers between devices: 65.3 us -> 102 us  [flipped(): return lax.ppermute(value, 'dp', [(i, i ^ flip) for i in range(count)])]
    add x14 -> x4, other arithmetic: 7.03 us -> 0.03 us  [body(): vector = vector + flipped(vector, flip)]
  transfers between devices with their start and end apart: 87 -> 86, of which waited for: 34 -> 39; matrix products, arithmetic and copies ran while one was open for 8% -> 4% of each run, Pallas kernels for 13% -> 42%
where the time goes in v2:
time: 608 us; the launch traced here: 599 us
  Pallas kernels  279 us (46%)
  waiting for transfers between devices  178 us (29%)
  starting transfers between devices  104 us (17%)
  other arithmetic  19.6 us (3%)
  local copies, waits for them, and re-layouts  17.2 us (3%)
    pallas_call x15, Pallas kernels, kernel_call(): pl.pallas_call(kernel, out_shape=outs, in_specs=[VM] * (len(args) - any_a...  279 us
    ppermute x70, waiting for transfers between devices, flipped(): return lax.ppermute(value, 'dp', [(i, i ^ flip) for i in range(count)])  174 us
    ppermute x70, starting transfers between devices, flipped(): return lax.ppermute(value, 'dp', [(i, i ^ flip) for i in range(count)])  102 us
  transfers between devices with their start and end apart: 86, of which 39 were waited for; matrix products, arithmetic and copies ran while one was open for 4% of the time, Pallas kernels for 42%

profile of v2, /device:TPU:0, one launch (start us, length us, event | category | flops | bytes accessed | tf_op | source)
XLA Modules:
  0.0 599.4 jit_solution(4266177125726523973)
XLA Ops:
  17.9 5.7 collective-permute-done.5
  28.1 5.9 collective-permute-done.18.far
  34.5 8.5 %collective-permute-done.12.refs_4_ = bf16[2,64,896]{2,1,0:T(8,128)(2,1)S(1)} collective-permute-done((bf16[2,64,896]{2,1,0:T(8,128)(2,1)S(1)}, bf16[2,64,896]{2,1,0:T(8,128)(2,1)S(1)}, u32[]{:S(2)}, u32[]{:S(2)}) %collective-permute-start.12) | collective-permute-done | bytes 229408 | tf_op jit(solution)/shard_map/ppermute | solution.py:432
  57.7 8.1 %collective-permute-done.15.refs_2_ = bf16[2,64,896]{2,1,0:T(8,128)(2,1)S(1)} collective-permute-done((bf16[2,64,896]{2,1,0:T(8,128)(2,1)S(1)}, bf16[2,64,896]{2,1,0:T(8,128)(2,1)S(1)}, u32[]{:S(2)}, u32[]{:S(2)}) %collective-permute-start.15) | collective-permute-done | bytes 229408 | tf_op jit(solution)/shard_map/ppermute | solution.py:432
  68.8 56.8 %join0_in.1.refs_10_.refs_9_ = bf16[1024,896]{1,0:T(8,128)(2,1)} custom-call(bf16[4,64,896]{2,1,0:T(8,128)(2,1)} %copy-done.17, bf16[2,64,896]{2,1,0:T(8,128)(2,1)} %copy-done.49, bf16[2,64,896]{2,1,0:T(8,128)(2,1)} %copy-done.50, bf16[4,64,896]{2,1,0:T(8,128)(2,1)} %copy-done.8, bf16[2,64,896]{2,1,0:T(8,128)(2,1)} %copy-done.45, bf16[2,64,896]{2,1,0:T(8,128)(2,1)} %copy-done.46), custom_call_target="tpu_custom_call" | custom-call | flops 1000000 | bytes 3670016 | tf_op jit(solution)/shard_map/join0_in/pallas_call | solution.py:397
  128.0 16.4 %collective-permute-done.37.far = bf16[320,512]{1,0:T(8,128)(2,1)S(1)} collective-permute-done((bf16[320,512]{1,0:T(8,128)(2,1)S(1)}, bf16[320,512]{1,0:T(8,128)(2,1)S(1)}, u32[]{:S(2)}, u32[]{:S(2)}) %collective-permute-start.37) | collective-permute-done | bytes 327712 | tf_op jit(solution)/shard_map/ppermute | solution.py:432
  147.4 40.9 %join0_out.1.refs_12_.refs_11_ = bf16[2,640,512]{2,1,0:T(8,128)(2,1)} custom-call(bf16[320,512]{1,0:T(8,128)(2,1)} %copy-done.11, bf16[320,512]{1,0:T(8,128)(2,1)} %copy-done.25, bf16[320,512]{1,0:T(8,128)(2,1)} %copy-done.24, bf16[320,512]{1,0:T(8,128)(2,1)} %copy-done.27), custom_call_target="tpu_custom_call" | custom-call | flops 1000000 | bytes 2621440 | tf_op jit(solution)/shard_map/join0_out/pallas_call | solution.py:397
  197.3 4.9 collective-permute-done.36.refs_1_
  202.3 56.8 %join1_in.1.refs_14_ = bf16[1024,896]{1,0:T(8,128)(2,1)} custom-call(bf16[4,64,896]{2,1,0:T(8,128)(2,1)} %copy-done.16, bf16[2,64,896]{2,1,0:T(8,128)(2,1)} %collective-permute-done.36.refs_1_, bf16[2,64,896]{2,1,0:T(8,128)(2,1)} %collective-permute-done.39.refs_2_, bf16[4,64,896]{2,1,0:T(8,128)(2,1)} %copy-done.9, bf16[2,64,896]{2,1,0:T(8,128)(2,1)} %copy-done.47, ...), custom_call_target="tpu_custom_call" | custom-call | flops 1000000 | bytes 3670016 | tf_op jit(solution)/shard_map/join1_in/pallas_call | solution.py:397
  262.7 6.8 %collective-permute-done.42.near_far = bf16[320,512]{1,0:T(8,128)(2,1)S(1)} collective-permute-done((bf16[320,512]{1,0:T(8,128)(2,1)S(1)}, bf16[320,512]{1,0:T(8,128)(2,1)S(1)}, u32[]{:S(2)}, u32[]{:S(2)}) %collective-permute-start.42) | collective-permute-done | bytes 327712 | tf_op jit(solution)/shard_map/ppermute | solution.py:432
  270.2 40.9 %join1_out.1.refs_16_ = bf16[2,640,512]{2,1,0:T(8,128)(2,1)} custom-call(bf16[320,512]{1,0:T(8,128)(2,1)} %copy-done.10, bf16[320,512]{1,0:T(8,128)(2,1)} %copy-done.26, bf16[320,512]{1,0:T(8,128)(2,1)} %copy-done.28, bf16[320,512]{1,0:T(8,128)(2,1)} %copy-done.29), custom_call_target="tpu_custom_call" | custom-call | flops 1000000 | bytes 2621440 | tf_op jit(solution)/shard_map/join1_out/pallas_call | solution.py:397
  311.8 11.4 %first_forward.1 = (f32[128,1024]{1,0:T(8,128)}, bf16[128,1024]{1,0:T(8,128)(2,1)}, bf16[128,1024]{1,0:T(8,128)(2,1)}, bf16[128,1024]{1,0:T(8,128)(2,1)}, bf16[5...) custom-call(bf16[144,1024]{1,0:T(8,128)(2,1)} %copy-done.32, ...), custom_call_target="tpu_custom_call" | custom-call | flops 3221225472 | bytes 15872000 | tf_op jit(solution)/shard_map/first_forward/pallas_call | solution.py:397
  323.2 7.2 %collective-permute-start.23 = (bf16[128,1024]{1,0:T(8,128)(2,1)}, bf16[128,1024]{1,0:T(8,128)(2,1)S(1)}, u32[]{:S(2)}, u32[]{:S(2)}) collective-permute-start(bf16[128,1024]{1,0:T(8,128)(2,1)} %get-tuple-element.123), channel_id=1, source_target_pairs={{0,4},{1,5},{2,6},{3,7},{4,0},{5,1},{6,2},{7,3},{8,12},{9,13},{10,... | collective-permute-start | bytes 786440 | tf_op jit(solution)/shard_map/ppermute | solution.py:432
  332.4 5.3 collective-permute-done.23
  347.6 4.3 collective-permute-start.27
  359.9 5.6 collective-permute-done.26.refs_2_
  366.3 18.0 %second_layer.1 = (f32[128,1024]{1,0:T(8,128)}, bf16[128,1024]{1,0:T(8,128)(2,1)}, bf16[128,1024]{1,0:T(8,128)(2,1)}, bf16[128,1024]{1,0:T(8,128)(2,1)}, f32[128...) custom-call(bf16[128,1024]{1,0:T(8,128)(2,1)} %copy-done.5, ...), custom_call_target="tpu_custom_call" | custom-call | flops 6442450944 | bytes 16531456 | tf_op jit(solution)/shard_map/second_layer/pallas_call | solution.py:397
  393.8 6.5 %grads1_out.1 = (bf16[2,320,512]{2,1,0:T(8,128)(2,1)}, bf16[2,320,512]{2,1,0:T(8,128)(2,1)}) custom-call(bf16[128,1024]{1,0:T(8,128)(2,1)} %copy-done.4, bf16[128,1024]{1,0:T(8,128)(2,1)} %copy-done.36, bf16[128,1024]{1,0:T(8,128)(2,1)} %copy-done.37, bf16[128,1024]{1,0:T(8,128)(2,1)} %copy-done.38, bf16[512,2304]{1,0:T(8,128)(2,1)} %get-tuple-element.139.refs_4_.ship_a, ...), custom_call_target="tpu_custom_call" | custom-call | flops 1610612736 | bytes 8519680 | tf_op jit(solution)/shard_map/grads1_out/pallas_call | solution.py:397
  400.2 7.1 %grads1_in.1 = (bf16[2,2,64,896]{3,2,1,0:T(8,128)(2,1)}, bf16[2,2,64,896]{3,2,1,0:T(8,128)(2,1)}, bf16[2,2,64,896]{3,2,1,0:T(8,128)(2,1)}, bf16[2,2,64,896]{3,2,1,0:T(8,128)(2,1)}) custom-call(bf16[512,2304]{1,0:T(8,128)(2,1)} %get-tuple-element.139.refs_4_.ship_a, bf16[512,2304]{1,0:T(8,128)(2,1)} %copy-done.1, bf16[512,896]{1,0:T(8,128)(2,1)} %get-tuple-element.143.gcat, ...), custom_call_target="tpu_custom_call" | custom-call | flops 1610612736 | bytes 8912896 | tf_op jit(solution)/shard_map/grads1_in/pallas_call | solution.py:397
  415.6 6.4 %collective-permute-done.51.refs_3_ = bf16[128,1024]{1,0:T(8,128)(2,1)S(1)} collective-permute-done((bf16[128,1024]{1,0:T(8,128)(2,1)}, bf16[128,1024]{1,0:T(8,128)(2,1)S(1)}, u32[]{:S(2)}, u32[]{:S(2)}) %collective-permute-start.51) | collective-permute-done | bytes 262176 | tf_op jit(solution)/shard_map/ppermute | solution.py:432
  422.0 4.7 collective-permute-done.50.refs_2_
  427.5 14.7 %first_backward.1 = (f32[128,1024]{1,0:T(8,128)}, bf16[128,1024]{1,0:T(8,128)(2,1)}, bf16[128,1024]{1,0:T(8,128)(2,1)}, bf16[128,1024]{1,0:T(8,128)(2,1)}, bf16[...) custom-call(bf16[128,1024]{1,0:T(8,128)(2,1)} %get-tuple-element.152.refs_0_.gout_ref, ...), custom_call_target="tpu_custom_call" | custom-call | flops 3221225472 | bytes 15470592 | tf_op jit(solution)/shard_map/first_backward/pallas_call | solution.py:397
  451.1 4.3 collective-permute-done.53.r2
  466.9 7.0 %collective-permute-done.60 = f32[16,448]{1,0:T(8,128)S(1)} collective-permute-done((f32[16,448]{1,0:T(8,128)S(1)}, f32[16,448]{1,0:T(8,128)S(1)}, u32[]{:S(2)}, u32[]{:S(2)}) %collective-permute-start.60) | collective-permute-done | bytes 28704 | tf_op jit(solution)/shard_map/ppermute | solution.py:432
  489.1 7.5 %collective-permute-done.57 = bf16[128,1024]{1,0:T(8,128)(2,1)S(1)} collective-permute-done((bf16[128,1024]{1,0:T(8,128)(2,1)}, bf16[128,1024]{1,0:T(8,128)(2,1)S(1)}, u32[]{:S(2)}, u32[]{:S(2)}) %collective-permute-start.57) | collective-permute-done | bytes 262176 | tf_op jit(solution)/shard_map/ppermute | solution.py:432
  503.6 8.3 %collective-permute-done.63 = f32[16,448]{1,0:T(8,128)S(1)} collective-permute-done((f32[16,448]{1,0:T(8,128)S(1)}, f32[16,448]{1,0:T(8,128)S(1)}, u32[]{:S(2)}, u32[]{:S(2)}) %collective-permute-start.63) | collective-permute-done | bytes 28704 | tf_op jit(solution)/shard_map/ppermute | solution.py:432
  513.6 7.0 %grads0_in.1 = (bf16[2,2,64,896]{3,2,1,0:T(8,128)(2,1)}, bf16[2,2,64,896]{3,2,1,0:T(8,128)(2,1)}, bf16[2,2,64,896]{3,2,1,0:T(8,128)(2,1)}, bf16[2,2,64,896]{3,2,1,0:T(8,128)(2,1)}) custom-call(bf16[512,2304]{1,0:T(8,128)(2,1)} %get-tuple-element.172.ship_a.refs_4_, bf16[512,2304]{1,0:T(8,128)(2,1)} %collective-permute-done.64.other_a.refs_5_, ...), custom_call_target="tpu_custom_call" | custom-call | flops 1610612736 | bytes 8912896 | tf_op jit(solution)/shard_map/grads0_in/pallas_call | solution.py:397
  523.8 6.2 %grads0_out.1 = (bf16[2,320,512]{2,1,0:T(8,128)(2,1)}, bf16[2,320,512]{2,1,0:T(8,128)(2,1)}) custom-call(bf16[128,1024]{1,0:T(8,128)(2,1)} %get-tuple-element.152.refs_0_.gout_ref, bf16[128,1024]{1,0:T(8,128)(2,1)} %copy-done.35, bf16[128,1024]{1,0:T(8,128)(2,1)} %copy-done.34, bf16[128,1024]{1,0:T(8,128)(2,1)} %copy-done.33, ...), custom_call_target="tpu_custom_call" | custom-call | flops 1610612736 | bytes 8519680 | tf_op jit(solution)/shard_map/grads0_out/pallas_call | solution.py:397
  537.6 6.4 %collective-permute-done.72 = bf16[2,2,64,896]{3,2,1,0:T(8,128)(2,1)S(1)} collective-permute-done((bf16[2,2,64,896]{3,2,1,0:T(8,128)(2,1)}, bf16[2,2,64,896]{3,2,1,0:T(8,128)(2,1)S(1)}, u32[]{:S(2)}, u32[]{:S(2)}) %collective-permute-start.72) | collective-permute-done | bytes 458784 | tf_op jit(solution)/shard_map/ppermute | solution.py:432
  547.0 10.6 %collective-permute-done.81 = bf16[2,320,512]{2,1,0:T(8,128)(2,1)S(1)} collective-permute-done((bf16[2,320,512]{2,1,0:T(8,128)(2,1)}, bf16[2,320,512]{2,1,0:T(8,128)(2,1)S(1)}, u32[]{:S(2)}, u32[]{:S(2)}) %collective-permute-start.81) | collective-permute-done | bytes 655392 | tf_op jit(solution)/shard_map/ppermute | solution.py:432
  562.5 8.2 %collective-permute-done.73 = bf16[2,64,896]{2,1,0:T(8,128)(2,1)S(1)} collective-permute-done((bf16[2,64,896]{2,1,0:T(8,128)(2,1)S(1)}, bf16[2,64,896]{2,1,0:T(8,128)(2,1)S(1)}, u32[]{:S(2)}, u32[]{:S(2)}) %collective-permute-start.73) | collective-permute-done | bytes 229408 | tf_op jit(solution)/shard_map/ppermute | solution.py:432
  583.1 5.0 collective-permute-done.74
  (396 shorter events, 183.9 us)
Async XLA Ops:
  23.7 22.8 %collective-permute-start.6 = (bf16[144,1024]{1,0:T(8,128)(2,1)S(1)}, bf16[144,1024]{1,0:T(8,128)(2,1)S(1)}, u32[]{:S(2)}, u32[]{:S(2)}) collective-permute-start(bf16[144,1024]{1,0:T(8,128)(2,1)S(1)} %pad_maximum_fusion.3.refs_0_), channel_id=1, source_target_pairs={{0,2},{1,3},{2,0},{3,1},{4,6},{5,7},{6,4},{7,5},{8,10},{9,11},{10,... | collective-permute-start | bytes 884744 | tf_op jit(solution)/shard_map/ppermute | solution.py:432
  24.3 22.2 %collective-permute-start.7 = (bf16[144,1024]{1,0:T(8,128)(2,1)S(1)}, bf16[144,1024]{1,0:T(8,128)(2,1)S(1)}, u32[]{:S(2)}, u32[]{:S(2)}) collective-permute-start(bf16[144,1024]{1,0:T(8,128)(2,1)S(1)} %pad_maximum_fusion.3.refs_0_), channel_id=1, source_target_pairs={{0,4},{1,5},{2,6},{3,7},{4,0},{5,1},{6,2},{7,3},{8,12},{9,13},{10,... | collective-permute-start | bytes 884744 | tf_op jit(solution)/shard_map/ppermute | solution.py:432
  24.3 23.0 %collective-permute-start.8 = (bf16[144,1024]{1,0:T(8,128)(2,1)S(1)}, bf16[144,1024]{1,0:T(8,128)(2,1)S(1)}, u32[]{:S(2)}, u32[]{:S(2)}) collective-permute-start(bf16[144,1024]{1,0:T(8,128)(2,1)S(1)} %pad_maximum_fusion.3.refs_0_), channel_id=1, source_target_pairs={{0,6},{1,7},{2,4},{3,5},{4,2},{5,3},{6,0},{7,1},{8,14},{9,15},{10,... | collective-permute-start | bytes 884744 | tf_op jit(solution)/shard_map/ppermute | solution.py:432
  34.0 19.0 %collective-permute-start.11 = (bf16[4,64,896]{2,1,0:T(8,128)(2,1)S(1)}, bf16[4,64,896]{2,1,0:T(8,128)(2,1)S(1)}, u32[]{:S(2)}, u32[]{:S(2)}) collective-permute-start(bf16[4,64,896]{2,1,0:T(8,128)(2,1)S(1)} %pad_maximum_fusion.refs_3_), channel_id=1, source_target_pairs={{0,1},{1,0},{2,3},{3,2},{4,5},{5,4},{6,7},{7,6},{8,9},{9,8},{10,11... | collective-permute-start | bytes 1376264 | tf_op jit(solution)/shard_map/ppermute | solution.py:432
  47.6 78.1 %collective-permute-start.31 = (bf16[64,896]{1,0:T(8,128)(2,1)S(1)}, bf16[64,896]{1,0:T(8,128)(2,1)S(1)}, u32[]{:S(2)}, u32[]{:S(2)}) collective-permute-start(bf16[64,896]{1,0:T(8,128)(2,1)S(1)} %get-tuple-element.128), channel_id=1, source_target_pairs={{0,2},{1,3},{2,0},{3,1},{4,6},{5,7},{6,4},{7,5},{8,10},{9,11},{10,... | collective-permute-start | bytes 344072 | tf_op jit(solution)/shard_map/ppermute | solution.py:432
  48.4 79.4 %collective-permute-start.32 = (bf16[64,896]{1,0:T(8,128)(2,1)S(1)}, bf16[64,896]{1,0:T(8,128)(2,1)S(1)}, u32[]{:S(2)}, u32[]{:S(2)}) collective-permute-start(bf16[64,896]{1,0:T(8,128)(2,1)S(1)} %get-tuple-element.129), channel_id=1, source_target_pairs={{0,4},{1,5},{2,6},{3,7},{4,0},{5,1},{6,2},{7,3},{8,12},{9,13},{10,... | collective-permute-start | bytes 344072 | tf_op jit(solution)/shard_map/ppermute | solution.py:432
  48.5 79.2 %collective-permute-start.33 = (bf16[64,896]{1,0:T(8,128)(2,1)S(1)}, bf16[64,896]{1,0:T(8,128)(2,1)S(1)}, u32[]{:S(2)}, u32[]{:S(2)}) collective-permute-start(bf16[64,896]{1,0:T(8,128)(2,1)S(1)} %get-tuple-element.130), channel_id=1, source_target_pairs={{0,6},{1,7},{2,4},{3,5},{4,2},{5,3},{6,0},{7,1},{8,14},{9,15},{10,... | collective-permute-start | bytes 344072 | tf_op jit(solution)/shard_map/ppermute | solution.py:432
  65.8 78.6 %collective-permute-start.20 = (bf16[320,512]{1,0:T(8,128)(2,1)S(1)}, bf16[320,512]{1,0:T(8,128)(2,1)S(1)}, u32[]{:S(2)}, u32[]{:S(2)}) collective-permute-start(bf16[320,512]{1,0:T(8,128)(2,1)S(1)} %collective-permute-done.18.far), channel_id=1, source_target_pairs={{0,1},{1,0},{2,3},{3,2},{4,5},{5,4},{6,7},{7,6},{8,9},{9,8},{10,11... | collective-permute-start | bytes 983048 | tf_op jit(solution)/shard_map/ppermute | solution.py:432
  67.8 120.4 %collective-permute-start.9 = (bf16[4,2,448]{2,1,0:T(2,128)(2,1)S(1)}, bf16[4,2,448]{2,1,0:T(2,128)(2,1)S(1)}, u32[]{:S(2)}, u32[]{:S(2)}) collective-permute-start(bf16[4,2,448]{2,1,0:T(2,128)(2,1)S(1)} %pad_maximum_fusion.10), channel_id=1, source_target_pairs={{0,8},{1,9},{2,10},{3,11},{4,12},{5,13},{6,14},{7,15},{8,0},{9,1},... | collective-permute-start | bytes 21512 | tf_op jit(solution)/shard_map/ppermute | solution.py:432
  127.7 184.0 %collective-permute-start.16 = (bf16[1024,896]{1,0:T(8,128)(2,1)}, bf16[1024,896]{1,0:T(8,128)(2,1)}, u32[]{:S(2)}, u32[]{:S(2)}) collective-permute-start(bf16[1024,896]{1,0:T(8,128)(2,1)} %join0_in.1.refs_10_.refs_9_), channel_id=1, source_target_pairs={{0,16},{16,0},{1,17},{17,1},{2,18},{18,2},{3,19},{19,3},{4,20},{20... | collective-permute-start | bytes 5505032 | tf_op jit(solution)/shard_map/ppermute | solution.py:427
  127.8 62.7 %collective-permute-start.34 = (bf16[4,64,896]{2,1,0:T(8,128)(2,1)S(1)}, bf16[4,64,896]{2,1,0:T(8,128)(2,1)S(1)}, u32[]{:S(2)}, u32[]{:S(2)}) collective-permute-start(bf16[4,64,896]{2,1,0:T(8,128)(2,1)S(1)} %pad_maximum_fusion.1.refs_3_), channel_id=1, source_target_pairs={{0,1},{1,0},{2,3},{3,2},{4,5},{5,4},{6,7},{7,6},{8,9},{9,8},{10,11... | collective-permute-start | bytes 1376264 | tf_op jit(solution)/shard_map/ppermute | solution.py:432
  144.4 44.0 %collective-permute-start.35 = (bf16[2,64,896]{2,1,0:T(8,128)(2,1)S(1)}, bf16[2,64,896]{2,1,0:T(8,128)(2,1)S(1)}, u32[]{:S(2)}, u32[]{:S(2)}) collective-permute-start(bf16[2,64,896]{2,1,0:T(8,128)(2,1)S(1)} %pad_maximum_fusion.6), channel_id=1, source_target_pairs={{0,8},{1,9},{2,10},{3,11},{4,12},{5,13},{6,14},{7,15},{8,0},{9,1},... | collective-permute-start | bytes 688136 | tf_op jit(solution)/shard_map/ppermute | solution.py:432
  144.4 44.0 %collective-permute-start.38 = (bf16[2,64,896]{2,1,0:T(8,128)(2,1)S(1)}, bf16[2,64,896]{2,1,0:T(8,128)(2,1)S(1)}, u32[]{:S(2)}, u32[]{:S(2)}) collective-permute-start(bf16[2,64,896]{2,1,0:T(8,128)(2,1)S(1)} %pad_maximum_fusion.7), channel_id=1, source_target_pairs={{0,8},{1,9},{2,10},{3,11},{4,12},{5,13},{6,14},{7,15},{8,0},{9,1},... | collective-permute-start | bytes 688136 | tf_op jit(solution)/shard_map/ppermute | solution.py:432
  188.3 123.5 %collective-permute-start.21 = (bf16[2,640,512]{2,1,0:T(8,128)(2,1)}, bf16[2,640,512]{2,1,0:T(8,128)(2,1)}, u32[]{:S(2)}, u32[]{:S(2)}) collective-permute-start(bf16[2,640,512]{2,1,0:T(8,128)(2,1)} %join0_out.1.refs_12_.refs_11_), channel_id=1, source_target_pairs={{0,16},{16,0},{1,17},{17,1},{2,18},{18,2},{3,19},{19,3},{4,20},{20... | collective-permute-start | bytes 3932168 | tf_op jit(solution)/shard_map/ppermute | solution.py:427
  192.6 66.7 %collective-permute-start.41 = (bf16[320,512]{1,0:T(8,128)(2,1)S(1)}, bf16[320,512]{1,0:T(8,128)(2,1)S(1)}, u32[]{:S(2)}, u32[]{:S(2)}) collective-permute-start(bf16[320,512]{1,0:T(8,128)(2,1)S(1)} %get-tuple-element.136.own), channel_id=1, source_target_pairs={{0,1},{1,0},{2,3},{3,2},{4,5},{5,4},{6,7},{7,6},{8,9},{9,8},{10,11... | collective-permute-start | bytes 983048 | tf_op jit(solution)/shard_map/ppermute | solution.py:432
  259.1 106.4 %collective-permute-start.40 = (bf16[1024,896]{1,0:T(8,128)(2,1)}, bf16[1024,896]{1,0:T(8,128)(2,1)}, u32[]{:S(2)}, u32[]{:S(2)}) collective-permute-start(bf16[1024,896]{1,0:T(8,128)(2,1)} %join1_in.1.refs_14_), channel_id=1, source_target_pairs={{0,16},{16,0},{1,17},{17,1},{2,18},{18,2},{3,19},{19,3},{4,20},{20... | collective-permute-start | bytes 5505032 | tf_op jit(solution)/shard_map/ppermute | solution.py:427
  311.1 47.2 %collective-permute-start.43 = (bf16[2,640,512]{2,1,0:T(8,128)(2,1)}, bf16[2,640,512]{2,1,0:T(8,128)(2,1)}, u32[]{:S(2)}, u32[]{:S(2)}) collective-permute-start(bf16[2,640,512]{2,1,0:T(8,128)(2,1)} %join1_out.1.refs_16_), channel_id=1, source_target_pairs={{0,16},{16,0},{1,17},{17,1},{2,18},{18,2},{3,19},{19,3},{4,20},{20... | collective-permute-start | bytes 3932168 | tf_op jit(solution)/shard_map/ppermute | solution.py:427
  384.9 22.4 %collective-permute-start.46 = (bf16[128,1024]{1,0:T(8,128)(2,1)}, bf16[128,1024]{1,0:T(8,128)(2,1)S(1)}, u32[]{:S(2)}, u32[]{:S(2)}) collective-permute-start(bf16[128,1024]{1,0:T(8,128)(2,1)} %get-tuple-element.149), channel_id=1, source_target_pairs={{0,2},{1,3},{2,0},{3,1},{4,6},{5,7},{6,4},{7,5},{8,10},{9,11},{10,... | collective-permute-start | bytes 786440 | tf_op jit(solution)/shard_map/ppermute | solution.py:432
  386.2 21.1 %collective-permute-start.47 = (bf16[128,1024]{1,0:T(8,128)(2,1)}, bf16[128,1024]{1,0:T(8,128)(2,1)S(1)}, u32[]{:S(2)}, u32[]{:S(2)}) collective-permute-start(bf16[128,1024]{1,0:T(8,128)(2,1)} %get-tuple-element.150), channel_id=1, source_target_pairs={{0,4},{1,5},{2,6},{3,7},{4,0},{5,1},{6,2},{7,3},{8,12},{9,13},{10,... | collective-permute-start | bytes 786440 | tf_op jit(solution)/shard_map/ppermute | solution.py:432
  388.0 19.4 %collective-permute-start.48 = (bf16[128,1024]{1,0:T(8,128)(2,1)}, bf16[128,1024]{1,0:T(8,128)(2,1)S(1)}, u32[]{:S(2)}, u32[]{:S(2)}) collective-permute-start(bf16[128,1024]{1,0:T(8,128)(2,1)} %get-tuple-element.151), channel_id=1, source_target_pairs={{0,6},{1,7},{2,4},{3,5},{4,2},{5,3},{6,0},{7,1},{8,14},{9,15},{10,... | collective-permute-start | bytes 786440 | tf_op jit(solution)/shard_map/ppermute | solution.py:432
  415.3 98.3 %collective-permute-start.64 = (bf16[512,2304]{1,0:T(8,128)(2,1)S(1)}, bf16[512,2304]{1,0:T(8,128)(2,1)}, u32[]{:S(2)}, u32[]{:S(2)}) collective-permute-start(bf16[512,2304]{1,0:T(8,128)(2,1)S(1)} %copy-done), channel_id=1, source_target_pairs={{0,16},{16,0},{1,17},{17,1},{2,18},{18,2},{3,19},{19,3},{4,20},{20... | collective-permute-start | bytes 7077896 | tf_op jit(solution)/shard_map/ppermute | solution.py:427
  443.6 30.3 %collective-permute-start.68 = (bf16[2,2,64,896]{3,2,1,0:T(8,128)(2,1)}, bf16[2,2,64,896]{3,2,1,0:T(8,128)(2,1)}, u32[]{:S(2)}, u32[]{:S(2)}) collective-permute-start(bf16[2,2,64,896]{3,2,1,0:T(8,128)(2,1)} %get-tuple-element.146), channel_id=1, source_target_pairs={{0,1},{1,0},{2,3},{3,2},{4,5},{5,4},{6,7},{7,6},{8,9},{9,8},{10,11... | collective-permute-start | bytes 1376264 | tf_op jit(solution)/shard_map/ppermute | solution.py:432
  450.7 25.1 %collective-permute-start.75 = (bf16[2,2,64,896]{3,2,1,0:T(8,128)(2,1)}, bf16[2,2,64,896]{3,2,1,0:T(8,128)(2,1)}, u32[]{:S(2)}, u32[]{:S(2)}) collective-permute-start(bf16[2,2,64,896]{3,2,1,0:T(8,128)(2,1)} %get-tuple-element.147), channel_id=1, source_target_pairs={{0,1},{1,0},{2,3},{3,2},{4,5},{5,4},{6,7},{7,6},{8,9},{9,8},{10,11... | collective-permute-start | bytes 1376264 | tf_op jit(solution)/shard_map/ppermute | solution.py:432
  473.9 39.8 %collective-permute-start.65 = (bf16[512,1408]{1,0:T(8,128)(2,1)}, bf16[512,1408]{1,0:T(8,128)(2,1)}, u32[]{:S(2)}, u32[]{:S(2)}) collective-permute-start(bf16[512,1408]{1,0:T(8,128)(2,1)} %get-tuple-element.174), channel_id=1, source_target_pairs={{0,16},{16,0},{1,17},{17,1},{2,18},{18,2},{3,19},{19,3},{4,20},{20... | collective-permute-start | bytes 4325384 | tf_op jit(solution)/shard_map/ppermute | solution.py:427
  475.8 24.8 %collective-permute-start.83 = (bf16[2,320,512]{2,1,0:T(8,128)(2,1)}, bf16[2,320,512]{2,1,0:T(8,128)(2,1)S(1)}, u32[]{:S(2)}, u32[]{:S(2)}) collective-permute-start(bf16[2,320,512]{2,1,0:T(8,128)(2,1)} %get-tuple-element.142), channel_id=1, source_target_pairs={{0,1},{1,0},{2,3},{3,2},{4,5},{5,4},{6,7},{7,6},{8,9},{9,8},{10,11... | collective-permute-start | bytes 1966088 | tf_op jit(solution)/shard_map/ppermute | solution.py:432
  486.9 25.7 %collective-permute-start.69 = (bf16[2,64,896]{2,1,0:T(8,128)(2,1)S(1)}, bf16[2,64,896]{2,1,0:T(8,128)(2,1)S(1)}, u32[]{:S(2)}, u32[]{:S(2)}) collective-permute-start(bf16[2,64,896]{2,1,0:T(8,128)(2,1)S(1)} %fusion.10), channel_id=1, source_target_pairs={{0,8},{1,9},{2,10},{3,11},{4,12},{5,13},{6,14},{7,15},{8,0},{9,1},... | collective-permute-start | bytes 688136 | tf_op jit(solution)/shard_map/ppermute | solution.py:432
  500.5 20.8 %collective-permute-start.76 = (bf16[2,64,896]{2,1,0:T(8,128)(2,1)}, bf16[2,64,896]{2,1,0:T(8,128)(2,1)S(1)}, u32[]{:S(2)}, u32[]{:S(2)}) collective-permute-start(bf16[2,64,896]{2,1,0:T(8,128)(2,1)} %fusion.12), channel_id=1, source_target_pairs={{0,8},{1,9},{2,10},{3,11},{4,12},{5,13},{6,14},{7,15},{8,0},{9,1},... | collective-permute-start | bytes 688136 | tf_op jit(solution)/shard_map/ppermute | solution.py:432
  511.9 81.7 %collective-permute-start.58 = (f32[128,1024]{1,0:T(8,128)S(1)}, f32[128,1024]{1,0:T(8,128)S(1)}, u32[]{:S(2)}, u32[]{:S(2)}) collective-permute-start(f32[128,1024]{1,0:T(8,128)S(1)} %get-tuple-element.185), channel_id=1, source_target_pairs={{0,16},{16,0},{1,17},{17,1},{2,18},{18,2},{3,19},{19,3},{4,20},{20... | collective-permute-start | bytes 1572872 | tf_op jit(solution)/shard_map/ppermute | solution.py:427
  512.6 76.3 %collective-permute-start.84 = (bf16[320,512]{1,0:T(8,128)(2,1)S(1)}, bf16[320,512]{1,0:T(8,128)(2,1)S(1)}, u32[]{:S(2)}, u32[]{:S(2)}) collective-permute-start(bf16[320,512]{1,0:T(8,128)(2,1)S(1)} %fusion.7), channel_id=1, source_target_pairs={{0,8},{1,9},{2,10},{3,11},{4,12},{5,13},{6,14},{7,15},{8,0},{9,1},... | collective-permute-start | bytes 983048 | tf_op jit(solution)/shard_map/ppermute | solution.py:432
  522.4 21.6 %collective-permute-start.72 = (bf16[2,2,64,896]{3,2,1,0:T(8,128)(2,1)}, bf16[2,2,64,896]{3,2,1,0:T(8,128)(2,1)S(1)}, u32[]{:S(2)}, u32[]{:S(2)}) collective-permute-start(bf16[2,2,64,896]{3,2,1,0:T(8,128)(2,1)} %get-tuple-element.178), channel_id=1, source_target_pairs={{0,1},{1,0},{2,3},{3,2},{4,5},{5,4},{6,7},{7,6},{8,9},{9,8},{10,11... | collective-permute-start | bytes 1376264 | tf_op jit(solution)/shard_map/ppermute | solution.py:432
  530.0 27.6 %collective-permute-start.81 = (bf16[2,320,512]{2,1,0:T(8,128)(2,1)}, bf16[2,320,512]{2,1,0:T(8,128)(2,1)S(1)}, u32[]{:S(2)}, u32[]{:S(2)}) collective-permute-start(bf16[2,320,512]{2,1,0:T(8,128)(2,1)} %get-tuple-element.180), channel_id=1, source_target_pairs={{0,1},{1,0},{2,3},{3,2},{4,5},{5,4},{6,7},{7,6},{8,9},{9,8},{10,11... | collective-permute-start | bytes 1966088 | tf_op jit(solution)/shard_map/ppermute | solution.py:432
  534.2 42.0 %collective-permute-start.79 = (bf16[64,896]{1,0:T(8,128)(2,1)S(1)}, bf16[64,896]{1,0:T(8,128)(2,1)S(1)}, u32[]{:S(2)}, u32[]{:S(2)}) collective-permute-start(bf16[64,896]{1,0:T(8,128)(2,1)S(1)} %get-tuple-element.219), channel_id=1, source_target_pairs={{0,6},{1,7},{2,4},{3,5},{4,2},{5,3},{6,0},{7,1},{8,14},{9,15},{10,... | collective-permute-start | bytes 344072 | tf_op jit(solution)/shard_map/ppermute | solution.py:432
  (115 other events, 2734.4 us)
